TPU v7x, 512 devices: a whole 4x8x8 slice. The times are simulated.
512 devices in a mesh: gx: 16 (over z, x_lo), gy: 32 (over y, x_hi, core).
Axes of the slice: x: 4 (x_hi: 2, x_lo: 2; x = x_hi * 2 + x_lo), y: 8, z: 8, core: 2. Of those that a mesh axis runs over, the one named last changes fastest.
Arguments:
- vectors: bfloat16 [2048, 32, 256], P(('gx', 'gy')), may hold values from -6 to 6
- leaf_basis: bfloat16 [2048, 256, 64], P(('gx', 'gy')), may hold values from -0.375 to 0.375
- near_blocks: bfloat16 [2048, 3, 256, 256], P(('gx', 'gy')), may hold values from -0.21875 to 0.21875
- near_index: int32 [2048, 3], P(('gx', 'gy')), may hold values from 0 to 2047, as said below
- near_count: int32 [2048], P(('gx', 'gy')), may hold values from 1 to 3, as said below
- leaf_couple: bfloat16 [2048, 6, 64, 64], P(('gx', 'gy')), may hold values from -0.3125 to 0.3125
- far_index: int32 [2048, 6], P(('gx', 'gy')), may hold values from 0 to 2047, as said below
- leaf_transfer: bfloat16 [2048, 64, 64], P(('gx', 'gy')), may hold values from -0.375 to 0.375
- level_couple: bfloat16 [3, 512, 4, 64, 64], P(None, ('gx', 'gy')), as said below
- level_transfer: bfloat16 [2, 512, 64, 64], P(None, ('gx', 'gy')), as said below
Outputs:
- result_field: float32 [2048, 32, 256], P(('gx', 'gy'))
Inputs may be any that keep to these rules, and one draw needn't show every extreme that they name: |near_index[t, j] - t| <= 8 for every leaf t, and this bound is reached. Slots j >= near_count[t] are padding; every device has a leaf with all 3 slots live. |far_index[t, j] - t| <= 8 for every leaf t, and this bound is reached. level_couple[k, a] equals level_couple[k, b] when a and b lie in one cluster of level k. level_transfer[k, a] equals level_transfer[k, b] when a and b lie in one cluster of level k.
All inputs are finite; a program needn't handle non-finite values.
Results may differ from a plain program's by a relative error of at most 0.0025.
Values may be sent and summed in bfloat16 or wider, within the bound.
A program may use at most 128 MiB of HBM per device.

v0:
```python
import jax
import jax.numpy as jnp
from jax import lax
from jax.sharding import PartitionSpec as P

UPL = 3


node_offsets = (-3, -2, 2, 3)


def passed_along(block, axis, distance):
    devices = range(lax.axis_size(axis))
    route = [(i - distance, i) for i in devices if i - distance in devices]
    return lax.ppermute(block, axis, route)


def swapped(value, axis, apart):
    mask = 2**apart
    pairs = [(source, source ^ mask) for source in range(lax.axis_size(axis))]
    return lax.ppermute(value, axis, pairs)


def batched_rows(gathered, matrices):
    leaves_dev, slots, rhs_count, width = gathered.shape
    flat_rows = gathered.transpose(0, 2, 1, 3).reshape(leaves_dev, rhs_count, slots * width)
    flat_mats = matrices.reshape(leaves_dev, slots * width, matrices.shape[-1])
    return lax.dot_general(
        flat_rows, flat_mats, (((2,), (1,)), ((0,), (0,))), preferred_element_type=jnp.float32
    )


def on_device(
    vectors,
    leaf_basis,
    near_blocks,
    near_index,
    near_count,
    leaf_couple,
    far_index,
    leaf_transfer,
    level_couple,
    level_transfer,
):
    highest = lax.Precision.HIGHEST
    leaves_dev = vectors.shape[0]
    near_slots = near_index.shape[1]
    coefficients = jnp.einsum(
        "trl,tlm->trm", vectors, leaf_basis, preferred_element_type=jnp.float32
    ).astype(jnp.bfloat16)
    fetched = {}
    for shift_by in (2, 1, -1, -2):
        fetched[shift_by] = passed_along((vectors, coefficients), ("gx", "gy"), shift_by)
    window_vectors = jnp.concatenate(
        [fetched[2][0], fetched[1][0], vectors, fetched[-1][0], fetched[-2][0]], axis=0
    )
    window_coeffs = jnp.concatenate(
        [fetched[2][1], fetched[1][1], coefficients, fetched[-1][1], fetched[-2][1]], axis=0
    )
    device = lax.axis_index(("gx", "gy"))
    first_leaf = (device - 2) * leaves_dev
    near_local = near_index - first_leaf
    far_local = far_index - first_leaf
    gathered = jnp.take(window_vectors, near_local, axis=0)
    live = jnp.arange(near_slots)[None, :] < near_count[:, None]
    gathered = jnp.where(live[:, :, None, None], gathered, jnp.zeros((), jnp.bfloat16))
    near_part = batched_rows(gathered, near_blocks)
    partner_coeffs = jnp.take(window_coeffs, far_local, axis=0)
    local_far = batched_rows(partner_coeffs, leaf_couple)
    upward = jnp.einsum(
        "lrm,lmn->rn", coefficients, leaf_transfer, preferred_element_type=jnp.float32
    )
    downs = []
    ups = []
    for height in range(UPL):
        ups.append(upward)
        if height < UPL - 1:
            contrib = jnp.dot(
                upward, level_transfer[height, 0].astype(jnp.float32), precision=highest
            )
            upward = contrib + swapped(contrib, ("gx", "gy"), height)
    for height in range(UPL):
        total = jnp.zeros_like(ups[height])
        for slot_id, offset in enumerate(node_offsets):
            distance = -offset * 2**height
            shifted = passed_along(ups[height], ("gx", "gy"), distance)
            total = total + jnp.dot(
                shifted, level_couple[height, 0, slot_id].astype(jnp.float32), precision=highest
            )
        downs.append(total)
    far_field = downs[UPL - 1]
    for height in reversed(range(UPL - 1)):
        far_field = downs[height] + jnp.dot(
            far_field, level_transfer[height, 0].astype(jnp.float32).T, precision=highest
        )
    leaf_part = jnp.einsum(
        "rp,lmp->lrm", far_field, leaf_transfer.astype(jnp.float32), precision=highest
    )
    field = (leaf_part + local_far).astype(jnp.bfloat16)
    far_out = jnp.einsum("lrm,lkm->lrk", field, leaf_basis, preferred_element_type=jnp.float32)
    return far_out + near_part


def solution(mesh):
    in_specs = (
        P(("gx", "gy"), None, None),
        P(("gx", "gy"), None, None),
        P(("gx", "gy"), None, None, None),
        P(("gx", "gy"), None),
        P(("gx", "gy")),
        P(("gx", "gy"), None, None, None),
        P(("gx", "gy"), None),
        P(("gx", "gy"), None, None),
        P(None, ("gx", "gy"), None, None, None),
        P(None, ("gx", "gy"), None, None),
    )
    out_specs = P(("gx", "gy"), None, None)
    return jax.shard_map(
        on_device, mesh=mesh, in_specs=in_specs, out_specs=out_specs, check_vma=False
    )
```

profile of v0, /device:TPU:256, one launch (start us, length us, event | category | flops | bytes accessed | tf_op | source)
XLA Modules:
  0.0 161.8 jit_solution(8158777301432871849)
XLA Ops:
  0.0 5.1 %collective-permute-start.18 = (bf16[4,32,256]{2,1,0:T(8,128)(2,1)}, bf16[4,32,256]{2,1,0:T(8,128)(2,1)S(1)}, u32[]{:S(2)}, u32[]{:S(2)}) collective-permute-start(bf16[4,32,256]{2,1,0:T(8,128)(2,1)} %param.10), channel_id=1, source_target_pairs={{0,2},{1,3},{2,4},{3,5},{4,6},{5,7},{6,8},{7,9},{8,10},{9,11},{10,... | collective-permute-start | bytes 196616 | tf_op jit(solution)/shard_map/ppermute | solution.py:15
  5.1 1.9 %collective-permute-start.19 = (bf16[4,32,256]{2,1,0:T(8,128)(2,1)}, bf16[4,32,256]{2,1,0:T(8,128)(2,1)S(1)}, u32[]{:S(2)}, u32[]{:S(2)}) collective-permute-start(bf16[4,32,256]{2,1,0:T(8,128)(2,1)} %param.10), channel_id=1, source_target_pairs={{0,1},{1,2},{2,3},{3,4},{4,5},{5,6},{6,7},{7,8},{8,9},{9,10},{10,1... | collective-permute-start | bytes 196616 | tf_op jit(solution)/shard_map/ppermute | solution.py:15
  7.0 9.1 %collective-permute-start.20 = (bf16[4,32,256]{2,1,0:T(8,128)(2,1)}, bf16[4,32,256]{2,1,0:T(8,128)(2,1)S(1)}, u32[]{:S(2)}, u32[]{:S(2)}) collective-permute-start(bf16[4,32,256]{2,1,0:T(8,128)(2,1)} %param.10), channel_id=1, source_target_pairs={{1,0},{2,1},{3,2},{4,3},{5,4},{6,5},{7,6},{8,7},{9,8},{10,9},{11,1... | collective-permute-start | bytes 196616 | tf_op jit(solution)/shard_map/ppermute | solution.py:15
  16.1 1.1 convolution_convert_fusion
  17.2 1.9 %collective-permute-start.14 = (bf16[4,32,64]{2,1,0:T(8,128)(2,1)S(1)}, bf16[4,32,64]{2,1,0:T(8,128)(2,1)S(1)}, u32[]{:S(2)}, u32[]{:S(2)}) collective-permute-start(bf16[4,32,64]{2,1,0:T(8,128)(2,1)S(1)} %convolution_convert_fusion), channel_id=1, source_target_pairs={{0,2},{1,3},{2,4},{3,5},{4,6},{5,7},{6,8},{7,9},{8,10},{9,11},{10,... | collective-permute-start | bytes 49160 | tf_op jit(solution)/shard_map/ppermute | solution.py:15
  19.1 1.0 convolution_bitcast_fusion.1
  20.2 0.8 fusion.34
  21.0 1.9 %collective-permute-start.4 = (f32[32,64]{1,0:T(8,128)S(1)}, f32[32,64]{1,0:T(8,128)S(1)}, u32[]{:S(2)}, u32[]{:S(2)}) collective-permute-start(f32[32,64]{1,0:T(8,128)S(1)} %fusion.34), channel_id=1, source_target_pairs={{0,1},{1,0},{2,3},{3,2},{4,5},{5,4},{6,7},{7,6},{8,9},{9,8},{10,11... | collective-permute-start | bytes 24584 | tf_op jit(solution)/shard_map/ppermute | solution.py:21
  22.9 0.7 compare_and_fusion
  23.7 0.7 iota_compare_fusion
  24.5 0.7 compare_and_fusion.1
  25.2 3.4 %collective-permute-start.3 = (f32[32,64]{1,0:T(8,128)S(1)}, f32[32,64]{1,0:T(8,128)S(1)}, u32[]{:S(2)}, u32[]{:S(2)}) collective-permute-start(f32[32,64]{1,0:T(8,128)S(1)} %convolution_bitcast_fusion.1), channel_id=1, source_target_pairs={{3,0},{4,1},{5,2},{6,3},{7,4},{8,5},{9,6},{10,7},{11,8},{12,9},{13... | collective-permute-start | bytes 24584 | tf_op jit(solution)/shard_map/ppermute | solution.py:15
  28.6 0.8 fusion.23
  29.5 2.3 %collective-permute-done.3 = f32[32,64]{1,0:T(8,128)S(1)} collective-permute-done((f32[32,64]{1,0:T(8,128)S(1)}, f32[32,64]{1,0:T(8,128)S(1)}, u32[]{:S(2)}, u32[]{:S(2)}) %collective-permute-start.3) | collective-permute-done | bytes 8224 | tf_op jit(solution)/shard_map/ppermute | solution.py:15
  31.8 13.3 %collective-permute-start.2 = (f32[32,64]{1,0:T(8,128)S(1)}, f32[32,64]{1,0:T(8,128)S(1)}, u32[]{:S(2)}, u32[]{:S(2)}) collective-permute-start(f32[32,64]{1,0:T(8,128)S(1)} %convolution_bitcast_fusion.1), channel_id=1, source_target_pairs={{2,0},{3,1},{4,2},{5,3},{6,4},{7,5},{8,6},{9,7},{10,8},{11,9},{12,... | collective-permute-start | bytes 24584 | tf_op jit(solution)/shard_map/ppermute | solution.py:15
  45.1 0.8 fusion.36
  45.9 0.6 collective-permute-done.2
  46.5 1.9 %collective-permute-start.1 = (f32[32,64]{1,0:T(8,128)S(1)}, f32[32,64]{1,0:T(8,128)S(1)}, u32[]{:S(2)}, u32[]{:S(2)}) collective-permute-start(f32[32,64]{1,0:T(8,128)S(1)} %convolution_bitcast_fusion.1), channel_id=1, source_target_pairs={{0,2},{1,3},{2,4},{3,5},{4,6},{5,7},{6,8},{7,9},{8,10},{9,11},{10,... | collective-permute-start | bytes 24584 | tf_op jit(solution)/shard_map/ppermute | solution.py:15
  48.4 0.8 fusion.38
  49.3 8.6 %collective-permute-done.1 = f32[32,64]{1,0:T(8,128)S(1)} collective-permute-done((f32[32,64]{1,0:T(8,128)S(1)}, f32[32,64]{1,0:T(8,128)S(1)}, u32[]{:S(2)}, u32[]{:S(2)}) %collective-permute-start.1) | collective-permute-done | bytes 8224 | tf_op jit(solution)/shard_map/ppermute | solution.py:15
  57.8 1.9 %collective-permute-start.15 = (bf16[4,32,64]{2,1,0:T(8,128)(2,1)S(1)}, bf16[4,32,64]{2,1,0:T(8,128)(2,1)S(1)}, u32[]{:S(2)}, u32[]{:S(2)}) collective-permute-start(bf16[4,32,64]{2,1,0:T(8,128)(2,1)S(1)} %convolution_convert_fusion), channel_id=1, source_target_pairs={{0,1},{1,2},{2,3},{3,4},{4,5},{5,6},{6,7},{7,8},{8,9},{9,10},{10,1... | collective-permute-start | bytes 49160 | tf_op jit(solution)/shard_map/ppermute | solution.py:15
  59.8 0.8 fusion.40
  60.6 9.1 %collective-permute-start.16 = (bf16[4,32,64]{2,1,0:T(8,128)(2,1)S(1)}, bf16[4,32,64]{2,1,0:T(8,128)(2,1)S(1)}, u32[]{:S(2)}, u32[]{:S(2)}) collective-permute-start(bf16[4,32,64]{2,1,0:T(8,128)(2,1)S(1)} %convolution_convert_fusion), channel_id=1, source_target_pairs={{1,0},{2,1},{3,2},{4,3},{5,4},{6,5},{7,6},{8,7},{9,8},{10,9},{11,1... | collective-permute-start | bytes 49160 | tf_op jit(solution)/shard_map/ppermute | solution.py:15
  69.7 1.9 %collective-permute-start.17 = (bf16[4,32,64]{2,1,0:T(8,128)(2,1)S(1)}, bf16[4,32,64]{2,1,0:T(8,128)(2,1)S(1)}, u32[]{:S(2)}, u32[]{:S(2)}) collective-permute-start(bf16[4,32,64]{2,1,0:T(8,128)(2,1)S(1)} %convolution_convert_fusion), channel_id=1, source_target_pairs={{2,0},{3,1},{4,2},{5,3},{6,4},{7,5},{8,6},{9,7},{10,8},{11,9},{12,... | collective-permute-start | bytes 49160 | tf_op jit(solution)/shard_map/ppermute | solution.py:15
  71.7 1.9 %collective-permute-start.8 = (f32[32,64]{1,0:T(8,128)S(1)}, f32[32,64]{1,0:T(8,128)S(1)}, u32[]{:S(2)}, u32[]{:S(2)}) collective-permute-start(f32[32,64]{1,0:T(8,128)S(1)} %add.60), channel_id=1, source_target_pairs={{6,0},{7,1},{8,2},{9,3},{10,4},{11,5},{12,6},{13,7},{14,8},{15,9},... | collective-permute-start | bytes 24584 | tf_op jit(solution)/shard_map/ppermute | solution.py:15
  73.6 3.4 %collective-permute-done.17 = bf16[4,32,64]{2,1,0:T(8,128)(2,1)S(1)} collective-permute-done((bf16[4,32,64]{2,1,0:T(8,128)(2,1)S(1)}, bf16[4,32,64]{2,1,0:T(8,128)(2,1)S(1)}, u32[]{:S(2)}, u32[]{:S(2)}) %collective-permute-start.17) | collective-permute-done | bytes 16416 | tf_op jit(solution)/shard_map/ppermute | solution.py:15
  77.0 1.9 %collective-permute-start.7 = (f32[32,64]{1,0:T(8,128)S(1)}, f32[32,64]{1,0:T(8,128)S(1)}, u32[]{:S(2)}, u32[]{:S(2)}) collective-permute-start(f32[32,64]{1,0:T(8,128)S(1)} %add.60), channel_id=1, source_target_pairs={{4,0},{5,1},{6,2},{7,3},{8,4},{9,5},{10,6},{11,7},{12,8},{13,9},{1... | collective-permute-start | bytes 24584 | tf_op jit(solution)/shard_map/ppermute | solution.py:15
  79.0 0.6 gather_fusion
  80.1 3.9 %collective-permute-start.6 = (f32[32,64]{1,0:T(8,128)S(1)}, f32[32,64]{1,0:T(8,128)S(1)}, u32[]{:S(2)}, u32[]{:S(2)}) collective-permute-start(f32[32,64]{1,0:T(8,128)S(1)} %add.60), channel_id=1, source_target_pairs={{0,4},{1,5},{2,6},{3,7},{4,8},{5,9},{6,10},{7,11},{8,12},{9,13},{1... | collective-permute-start | bytes 24584 | tf_op jit(solution)/shard_map/ppermute | solution.py:15
  84.1 5.3 %collective-permute-start.9 = (f32[32,64]{1,0:T(8,128)S(1)}, f32[32,64]{1,0:T(8,128)S(1)}, u32[]{:S(2)}, u32[]{:S(2)}) collective-permute-start(f32[32,64]{1,0:T(8,128)S(1)} %fusion.23), channel_id=1, source_target_pairs={{0,2},{1,3},{2,0},{3,1},{4,6},{5,7},{6,4},{7,5},{8,10},{9,11},{10,... | collective-permute-start | bytes 24584 | tf_op jit(solution)/shard_map/ppermute | solution.py:21
  89.6 1.7 %collective-permute-done.9 = f32[32,64]{1,0:T(8,128)S(1)} collective-permute-done((f32[32,64]{1,0:T(8,128)S(1)}, f32[32,64]{1,0:T(8,128)S(1)}, u32[]{:S(2)}, u32[]{:S(2)}) %collective-permute-start.9) | collective-permute-done | bytes 8224 | tf_op jit(solution)/shard_map/ppermute | solution.py:21
  91.3 10.1 %collective-permute-start.21 = (bf16[4,32,256]{2,1,0:T(8,128)(2,1)S(1)}, bf16[4,32,256]{2,1,0:T(8,128)(2,1)S(1)}, u32[]{:S(2)}, u32[]{:S(2)}) collective-permute-start(bf16[4,32,256]{2,1,0:T(8,128)(2,1)S(1)} %copy-done.3), channel_id=1, source_target_pairs={{2,0},{3,1},{4,2},{5,3},{6,4},{7,5},{8,6},{9,7},{10,8},{11,9},{12,... | collective-permute-start | bytes 196616 | tf_op jit(solution)/shard_map/ppermute | solution.py:15
  101.4 1.9 %collective-permute-start.13 = (f32[32,64]{1,0:T(8,128)S(1)}, f32[32,64]{1,0:T(8,128)S(1)}, u32[]{:S(2)}, u32[]{:S(2)}) collective-permute-start(f32[32,64]{1,0:T(8,128)S(1)} %add.64), channel_id=1, source_target_pairs={{12,0},{13,1},{14,2},{15,3},{16,4},{17,5},{18,6},{19,7},{20,8},{21... | collective-permute-start | bytes 24584 | tf_op jit(solution)/shard_map/ppermute | solution.py:15
  103.4 5.4 %collective-permute-done.13 = f32[32,64]{1,0:T(8,128)S(1)} collective-permute-done((f32[32,64]{1,0:T(8,128)S(1)}, f32[32,64]{1,0:T(8,128)S(1)}, u32[]{:S(2)}, u32[]{:S(2)}) %collective-permute-start.13) | collective-permute-done | bytes 8224 | tf_op jit(solution)/shard_map/ppermute | solution.py:15
  108.8 1.9 %collective-permute-start.12 = (f32[32,64]{1,0:T(8,128)S(1)}, f32[32,64]{1,0:T(8,128)S(1)}, u32[]{:S(2)}, u32[]{:S(2)}) collective-permute-start(f32[32,64]{1,0:T(8,128)S(1)} %add.64), channel_id=1, source_target_pairs={{8,0},{9,1},{10,2},{11,3},{12,4},{13,5},{14,6},{15,7},{16,8},{17,9... | collective-permute-start | bytes 24584 | tf_op jit(solution)/shard_map/ppermute | solution.py:15
  110.9 4.5 %collective-permute-done.12 = f32[32,64]{1,0:T(8,128)S(1)} collective-permute-done((f32[32,64]{1,0:T(8,128)S(1)}, f32[32,64]{1,0:T(8,128)S(1)}, u32[]{:S(2)}, u32[]{:S(2)}) %collective-permute-start.12) | collective-permute-done | bytes 8224 | tf_op jit(solution)/shard_map/ppermute | solution.py:15
  115.4 1.9 %collective-permute-start.11 = (f32[32,64]{1,0:T(8,128)S(1)}, f32[32,64]{1,0:T(8,128)S(1)}, u32[]{:S(2)}, u32[]{:S(2)}) collective-permute-start(f32[32,64]{1,0:T(8,128)S(1)} %add.64), channel_id=1, source_target_pairs={{0,8},{1,9},{2,10},{3,11},{4,12},{5,13},{6,14},{7,15},{8,16},{9,17... | collective-permute-start | bytes 24584 | tf_op jit(solution)/shard_map/ppermute | solution.py:15
  117.4 8.7 %collective-permute-done.11 = f32[32,64]{1,0:T(8,128)S(1)} collective-permute-done((f32[32,64]{1,0:T(8,128)S(1)}, f32[32,64]{1,0:T(8,128)S(1)}, u32[]{:S(2)}, u32[]{:S(2)}) %collective-permute-start.11) | collective-permute-done | bytes 8224 | tf_op jit(solution)/shard_map/ppermute | solution.py:15
  126.1 1.9 %collective-permute-start.10 = (f32[32,64]{1,0:T(8,128)S(1)}, f32[32,64]{1,0:T(8,128)S(1)}, u32[]{:S(2)}, u32[]{:S(2)}) collective-permute-start(f32[32,64]{1,0:T(8,128)S(1)} %add.64), channel_id=1, source_target_pairs={{0,12},{1,13},{2,14},{3,15},{4,16},{5,17},{6,18},{7,19},{8,20},{9,... | collective-permute-start | bytes 24584 | tf_op jit(solution)/shard_map/ppermute | solution.py:15
  128.2 9.6 %collective-permute-done.10 = f32[32,64]{1,0:T(8,128)S(1)} collective-permute-done((f32[32,64]{1,0:T(8,128)S(1)}, f32[32,64]{1,0:T(8,128)S(1)}, u32[]{:S(2)}, u32[]{:S(2)}) %collective-permute-start.10) | collective-permute-done | bytes 8224 | tf_op jit(solution)/shard_map/ppermute | solution.py:15
  137.8 5.6 %collective-permute-start.5 = (f32[32,64]{1,0:T(8,128)S(1)}, f32[32,64]{1,0:T(8,128)S(1)}, u32[]{:S(2)}, u32[]{:S(2)}) collective-permute-start(f32[32,64]{1,0:T(8,128)S(1)} %add.60), channel_id=1, source_target_pairs={{0,6},{1,7},{2,8},{3,9},{4,10},{5,11},{6,12},{7,13},{8,14},{9,15},... | collective-permute-start | bytes 24584 | tf_op jit(solution)/shard_map/ppermute | solution.py:15
  143.7 6.0 %collective-permute-done.5 = f32[32,64]{1,0:T(8,128)S(1)} collective-permute-done((f32[32,64]{1,0:T(8,128)S(1)}, f32[32,64]{1,0:T(8,128)S(1)}, u32[]{:S(2)}, u32[]{:S(2)}) %collective-permute-start.5) | collective-permute-done | bytes 8224 | tf_op jit(solution)/shard_map/ppermute | solution.py:15
  149.8 1.9 %collective-permute-start = (f32[32,64]{1,0:T(8,128)S(1)}, f32[32,64]{1,0:T(8,128)S(1)}, u32[]{:S(2)}, u32[]{:S(2)}) collective-permute-start(f32[32,64]{1,0:T(8,128)S(1)} %convolution_bitcast_fusion.1), channel_id=1, source_target_pairs={{0,3},{1,4},{2,5},{3,6},{4,7},{5,8},{6,9},{7,10},{8,11},{9,12},{10... | collective-permute-start | bytes 24584 | tf_op jit(solution)/shard_map/ppermute | solution.py:15
  151.9 7.1 %collective-permute-done = f32[32,64]{1,0:T(8,128)S(1)} collective-permute-done((f32[32,64]{1,0:T(8,128)S(1)}, f32[32,64]{1,0:T(8,128)S(1)}, u32[]{:S(2)}, u32[]{:S(2)}) %collective-permute-start) | collective-permute-done | bytes 8224 | tf_op jit(solution)/shard_map/ppermute | solution.py:15
  159.2 0.3 fusion.1
  159.6 0.6 gather_fusion.1
  160.6 0.4 fusion.60
  161.0 0.8 convolution_add_fusion
  (57 shorter events, 2.6 us)
Async XLA Ops:
  0.0 160.6 %copy-start = (bf16[4,3,256,256]{3,2,1,0:T(8,128)(2,1)S(1)}, bf16[4,3,256,256]{3,2,1,0:T(8,128)(2,1)}, u32[]{:S(2)}) copy-start(bf16[4,3,256,256]{3,2,1,0:T(8,128)(2,1)} %param.12) | copy-start | bytes 4718596
  0.0 91.3 %copy-start.3 = (bf16[4,32,256]{2,1,0:T(8,128)(2,1)S(1)}, bf16[4,32,256]{2,1,0:T(8,128)(2,1)}, u32[]{:S(2)}) copy-start(bf16[4,32,256]{2,1,0:T(8,128)(2,1)} %param.10) | copy-start | bytes 196612
  0.0 143.6 %copy-start.6 = (bf16[2,1,64,64]{3,2,1,0:T(8,128)(2,1)S(1)}, bf16[2,1,64,64]{3,2,1,0:T(8,128)(2,1)}, u32[]{:S(2)}) copy-start(bf16[2,1,64,64]{3,2,1,0:T(8,128)(2,1)} %param.19) | copy-start | bytes 49156
  0.0 84.0 %copy-start.5 = (bf16[3,1,4,64,64]{4,3,2,1,0:T(8,128)(2,1)S(1)}, bf16[3,1,4,64,64]{4,3,2,1,0:T(8,128)(2,1)}, u32[]{:S(2)}) copy-start(bf16[3,1,4,64,64]{4,3,2,1,0:T(8,128)(2,1)} %param.18) | copy-start | bytes 294916
  0.0 79.8 %copy-start.2 = (bf16[4,6,64,64]{3,2,1,0:T(8,128)(2,1)S(1)}, bf16[4,6,64,64]{3,2,1,0:T(8,128)(2,1)}, u32[]{:S(2)}) copy-start(bf16[4,6,64,64]{3,2,1,0:T(8,128)(2,1)} %param.15) | copy-start | bytes 589828
  0.0 159.4 %collective-permute-start.18 = (bf16[4,32,256]{2,1,0:T(8,128)(2,1)}, bf16[4,32,256]{2,1,0:T(8,128)(2,1)S(1)}, u32[]{:S(2)}, u32[]{:S(2)}) collective-permute-start(bf16[4,32,256]{2,1,0:T(8,128)(2,1)} %param.10), channel_id=1, source_target_pairs={{0,2},{1,3},{2,4},{3,5},{4,6},{5,7},{6,8},{7,9},{8,10},{9,11},{10,... | collective-permute-start | bytes 196616 | tf_op jit(solution)/shard_map/ppermute | solution.py:15
  5.1 154.4 %collective-permute-start.19 = (bf16[4,32,256]{2,1,0:T(8,128)(2,1)}, bf16[4,32,256]{2,1,0:T(8,128)(2,1)S(1)}, u32[]{:S(2)}, u32[]{:S(2)}) collective-permute-start(bf16[4,32,256]{2,1,0:T(8,128)(2,1)} %param.10), channel_id=1, source_target_pairs={{0,1},{1,2},{2,3},{3,4},{4,5},{5,6},{6,7},{7,8},{8,9},{9,10},{10,1... | collective-permute-start | bytes 196616 | tf_op jit(solution)/shard_map/ppermute | solution.py:15
  7.0 152.5 %collective-permute-start.20 = (bf16[4,32,256]{2,1,0:T(8,128)(2,1)}, bf16[4,32,256]{2,1,0:T(8,128)(2,1)S(1)}, u32[]{:S(2)}, u32[]{:S(2)}) collective-permute-start(bf16[4,32,256]{2,1,0:T(8,128)(2,1)} %param.10), channel_id=1, source_target_pairs={{1,0},{2,1},{3,2},{4,3},{5,4},{6,5},{7,6},{8,7},{9,8},{10,9},{11,1... | collective-permute-start | bytes 196616 | tf_op jit(solution)/shard_map/ppermute | solution.py:15
  17.2 43.4 %collective-permute-start.14 = (bf16[4,32,64]{2,1,0:T(8,128)(2,1)S(1)}, bf16[4,32,64]{2,1,0:T(8,128)(2,1)S(1)}, u32[]{:S(2)}, u32[]{:S(2)}) collective-permute-start(bf16[4,32,64]{2,1,0:T(8,128)(2,1)S(1)} %convolution_convert_fusion), channel_id=1, source_target_pairs={{0,2},{1,3},{2,4},{3,5},{4,6},{5,7},{6,8},{7,9},{8,10},{9,11},{10,... | collective-permute-start | bytes 49160 | tf_op jit(solution)/shard_map/ppermute | solution.py:15
  21.0 4.2 %collective-permute-start.4 = (f32[32,64]{1,0:T(8,128)S(1)}, f32[32,64]{1,0:T(8,128)S(1)}, u32[]{:S(2)}, u32[]{:S(2)}) collective-permute-start(f32[32,64]{1,0:T(8,128)S(1)} %fusion.34), channel_id=1, source_target_pairs={{0,1},{1,0},{2,3},{3,2},{4,5},{5,4},{6,7},{7,6},{8,9},{9,8},{10,11... | collective-permute-start | bytes 24584 | tf_op jit(solution)/shard_map/ppermute | solution.py:21
  23.6 135.5 %copy-start.4 = (bf16[4,64,64]{2,1,0:T(8,128)(2,1)S(1)}, bf16[4,64,64]{2,1,0:T(8,128)(2,1)}, u32[]{:S(2)}) copy-start(bf16[4,64,64]{2,1,0:T(8,128)(2,1)} %param.17) | copy-start | bytes 98308
  25.2 6.6 %collective-permute-start.3 = (f32[32,64]{1,0:T(8,128)S(1)}, f32[32,64]{1,0:T(8,128)S(1)}, u32[]{:S(2)}, u32[]{:S(2)}) collective-permute-start(f32[32,64]{1,0:T(8,128)S(1)} %convolution_bitcast_fusion.1), channel_id=1, source_target_pairs={{3,0},{4,1},{5,2},{6,3},{7,4},{8,5},{9,6},{10,7},{11,8},{12,9},{13... | collective-permute-start | bytes 24584 | tf_op jit(solution)/shard_map/ppermute | solution.py:15
  31.8 14.7 %collective-permute-start.2 = (f32[32,64]{1,0:T(8,128)S(1)}, f32[32,64]{1,0:T(8,128)S(1)}, u32[]{:S(2)}, u32[]{:S(2)}) collective-permute-start(f32[32,64]{1,0:T(8,128)S(1)} %convolution_bitcast_fusion.1), channel_id=1, source_target_pairs={{2,0},{3,1},{4,2},{5,3},{6,4},{7,5},{8,6},{9,7},{10,8},{11,9},{12,... | collective-permute-start | bytes 24584 | tf_op jit(solution)/shard_map/ppermute | solution.py:15
  46.5 11.3 %collective-permute-start.1 = (f32[32,64]{1,0:T(8,128)S(1)}, f32[32,64]{1,0:T(8,128)S(1)}, u32[]{:S(2)}, u32[]{:S(2)}) collective-permute-start(f32[32,64]{1,0:T(8,128)S(1)} %convolution_bitcast_fusion.1), channel_id=1, source_target_pairs={{0,2},{1,3},{2,4},{3,5},{4,6},{5,7},{6,8},{7,9},{8,10},{9,11},{10,... | collective-permute-start | bytes 24584 | tf_op jit(solution)/shard_map/ppermute | solution.py:15
  57.8 11.9 %collective-permute-start.15 = (bf16[4,32,64]{2,1,0:T(8,128)(2,1)S(1)}, bf16[4,32,64]{2,1,0:T(8,128)(2,1)S(1)}, u32[]{:S(2)}, u32[]{:S(2)}) collective-permute-start(bf16[4,32,64]{2,1,0:T(8,128)(2,1)S(1)} %convolution_convert_fusion), channel_id=1, source_target_pairs={{0,1},{1,2},{2,3},{3,4},{4,5},{5,6},{6,7},{7,8},{8,9},{9,10},{10,1... | collective-permute-start | bytes 49160 | tf_op jit(solution)/shard_map/ppermute | solution.py:15
  60.6 11.1 %collective-permute-start.16 = (bf16[4,32,64]{2,1,0:T(8,128)(2,1)S(1)}, bf16[4,32,64]{2,1,0:T(8,128)(2,1)S(1)}, u32[]{:S(2)}, u32[]{:S(2)}) collective-permute-start(bf16[4,32,64]{2,1,0:T(8,128)(2,1)S(1)} %convolution_convert_fusion), channel_id=1, source_target_pairs={{1,0},{2,1},{3,2},{4,3},{5,4},{6,5},{7,6},{8,7},{9,8},{10,9},{11,1... | collective-permute-start | bytes 49160 | tf_op jit(solution)/shard_map/ppermute | solution.py:15
  69.7 7.3 %collective-permute-start.17 = (bf16[4,32,64]{2,1,0:T(8,128)(2,1)S(1)}, bf16[4,32,64]{2,1,0:T(8,128)(2,1)S(1)}, u32[]{:S(2)}, u32[]{:S(2)}) collective-permute-start(bf16[4,32,64]{2,1,0:T(8,128)(2,1)S(1)} %convolution_convert_fusion), channel_id=1, source_target_pairs={{2,0},{3,1},{4,2},{5,3},{6,4},{7,5},{8,6},{9,7},{10,8},{11,9},{12,... | collective-permute-start | bytes 49160 | tf_op jit(solution)/shard_map/ppermute | solution.py:15
  71.7 8.4 %collective-permute-start.8 = (f32[32,64]{1,0:T(8,128)S(1)}, f32[32,64]{1,0:T(8,128)S(1)}, u32[]{:S(2)}, u32[]{:S(2)}) collective-permute-start(f32[32,64]{1,0:T(8,128)S(1)} %add.60), channel_id=1, source_target_pairs={{6,0},{7,1},{8,2},{9,3},{10,4},{11,5},{12,6},{13,7},{14,8},{15,9},... | collective-permute-start | bytes 24584 | tf_op jit(solution)/shard_map/ppermute | solution.py:15
  77.0 7.1 %collective-permute-start.7 = (f32[32,64]{1,0:T(8,128)S(1)}, f32[32,64]{1,0:T(8,128)S(1)}, u32[]{:S(2)}, u32[]{:S(2)}) collective-permute-start(f32[32,64]{1,0:T(8,128)S(1)} %add.60), channel_id=1, source_target_pairs={{4,0},{5,1},{6,2},{7,3},{8,4},{9,5},{10,6},{11,7},{12,8},{13,9},{1... | collective-permute-start | bytes 24584 | tf_op jit(solution)/shard_map/ppermute | solution.py:15
  80.1 21.3 %collective-permute-start.6 = (f32[32,64]{1,0:T(8,128)S(1)}, f32[32,64]{1,0:T(8,128)S(1)}, u32[]{:S(2)}, u32[]{:S(2)}) collective-permute-start(f32[32,64]{1,0:T(8,128)S(1)} %add.60), channel_id=1, source_target_pairs={{0,4},{1,5},{2,6},{3,7},{4,8},{5,9},{6,10},{7,11},{8,12},{9,13},{1... | collective-permute-start | bytes 24584 | tf_op jit(solution)/shard_map/ppermute | solution.py:15
  84.1 7.1 %collective-permute-start.9 = (f32[32,64]{1,0:T(8,128)S(1)}, f32[32,64]{1,0:T(8,128)S(1)}, u32[]{:S(2)}, u32[]{:S(2)}) collective-permute-start(f32[32,64]{1,0:T(8,128)S(1)} %fusion.23), channel_id=1, source_target_pairs={{0,2},{1,3},{2,0},{3,1},{4,6},{5,7},{6,4},{7,5},{8,10},{9,11},{10,... | collective-permute-start | bytes 24584 | tf_op jit(solution)/shard_map/ppermute | solution.py:21
  91.3 68.3 %collective-permute-start.21 = (bf16[4,32,256]{2,1,0:T(8,128)(2,1)S(1)}, bf16[4,32,256]{2,1,0:T(8,128)(2,1)S(1)}, u32[]{:S(2)}, u32[]{:S(2)}) collective-permute-start(bf16[4,32,256]{2,1,0:T(8,128)(2,1)S(1)} %copy-done.3), channel_id=1, source_target_pairs={{2,0},{3,1},{4,2},{5,3},{6,4},{7,5},{8,6},{9,7},{10,8},{11,9},{12,... | collective-permute-start | bytes 196616 | tf_op jit(solution)/shard_map/ppermute | solution.py:15
  101.4 7.5 %collective-permute-start.13 = (f32[32,64]{1,0:T(8,128)S(1)}, f32[32,64]{1,0:T(8,128)S(1)}, u32[]{:S(2)}, u32[]{:S(2)}) collective-permute-start(f32[32,64]{1,0:T(8,128)S(1)} %add.64), channel_id=1, source_target_pairs={{12,0},{13,1},{14,2},{15,3},{16,4},{17,5},{18,6},{19,7},{20,8},{21... | collective-permute-start | bytes 24584 | tf_op jit(solution)/shard_map/ppermute | solution.py:15
  108.8 6.5 %collective-permute-start.12 = (f32[32,64]{1,0:T(8,128)S(1)}, f32[32,64]{1,0:T(8,128)S(1)}, u32[]{:S(2)}, u32[]{:S(2)}) collective-permute-start(f32[32,64]{1,0:T(8,128)S(1)} %add.64), channel_id=1, source_target_pairs={{8,0},{9,1},{10,2},{11,3},{12,4},{13,5},{14,6},{15,7},{16,8},{17,9... | collective-permute-start | bytes 24584 | tf_op jit(solution)/shard_map/ppermute | solution.py:15
  115.4 10.7 %collective-permute-start.11 = (f32[32,64]{1,0:T(8,128)S(1)}, f32[32,64]{1,0:T(8,128)S(1)}, u32[]{:S(2)}, u32[]{:S(2)}) collective-permute-start(f32[32,64]{1,0:T(8,128)S(1)} %add.64), channel_id=1, source_target_pairs={{0,8},{1,9},{2,10},{3,11},{4,12},{5,13},{6,14},{7,15},{8,16},{9,17... | collective-permute-start | bytes 24584 | tf_op jit(solution)/shard_map/ppermute | solution.py:15
  126.1 11.7 %collective-permute-start.10 = (f32[32,64]{1,0:T(8,128)S(1)}, f32[32,64]{1,0:T(8,128)S(1)}, u32[]{:S(2)}, u32[]{:S(2)}) collective-permute-start(f32[32,64]{1,0:T(8,128)S(1)} %add.64), channel_id=1, source_target_pairs={{0,12},{1,13},{2,14},{3,15},{4,16},{5,17},{6,18},{7,19},{8,20},{9,... | collective-permute-start | bytes 24584 | tf_op jit(solution)/shard_map/ppermute | solution.py:15
  137.8 11.9 %collective-permute-start.5 = (f32[32,64]{1,0:T(8,128)S(1)}, f32[32,64]{1,0:T(8,128)S(1)}, u32[]{:S(2)}, u32[]{:S(2)}) collective-permute-start(f32[32,64]{1,0:T(8,128)S(1)} %add.60), channel_id=1, source_target_pairs={{0,6},{1,7},{2,8},{3,9},{4,10},{5,11},{6,12},{7,13},{8,14},{9,15},... | collective-permute-start | bytes 24584 | tf_op jit(solution)/shard_map/ppermute | solution.py:15
  149.8 9.3 %collective-permute-start = (f32[32,64]{1,0:T(8,128)S(1)}, f32[32,64]{1,0:T(8,128)S(1)}, u32[]{:S(2)}, u32[]{:S(2)}) collective-permute-start(f32[32,64]{1,0:T(8,128)S(1)} %convolution_bitcast_fusion.1), channel_id=1, source_target_pairs={{0,3},{1,4},{2,5},{3,6},{4,7},{5,8},{6,9},{7,10},{8,11},{9,12},{10... | collective-permute-start | bytes 24584 | tf_op jit(solution)/shard_map/ppermute | solution.py:15
  159.6 1.4 copy-start.1
where the time goes:
time: 163 us; the launch traced here: 162 us
  starting transfers between devices  89.6 us (55%)
  waiting for transfers between devices  58 us (36%)
  matrix products  9.34 us (6%)
  other arithmetic  2.45 us (2%)
  local copies, waits for them, and re-layouts  1.85 us (1%)
    ppermute x20, starting transfers between devices, passed_along(): return lax.ppermute(block, axis, route)  82.4 us
    ppermute x20, waiting for transfers between devices, passed_along(): return lax.ppermute(block, axis, route)  56.3 us
    ppermute x2, starting transfers between devices, swapped(): return lax.ppermute(value, axis, pairs)  7.22 us
    dot_general x12, matrix products, on_device(): jnp.dot(shifted, level_couple[height, 0, slot_id].astype(jnp.float32), pr...  3.66 us
  transfers between devices with their start and end apart: 22, of which 11 were waited for; matrix products, arithmetic and copies ran while one was open for 7% of the time, Pallas kernels for 0%

commit v1 on v0

v1 whole, which is shorter than its diff:
```python
import jax
import jax.numpy as jnp
from jax import lax
from jax.experimental import pallas as pl
from jax.experimental.pallas import tpu as pltpu
from jax.sharding import PartitionSpec as P

MESH = pl.DeviceIdType.MESH
NODES = 512
OFFSETS = (-3, -2, 2, 3)
NEAR_OFFSETS = (-2, -1, 1, 2)
F32, BF16 = jnp.float32, jnp.bfloat16


def split(x):
    high = x.astype(BF16)
    return high, (x - high.astype(F32)).astype(BF16)


def dot(a, b):
    return jnp.dot(a, b, preferred_element_type=F32)


def dot_t(a, b):
    return lax.dot_general(a, b, (((1,), (1,)), ((), ())), preferred_element_type=F32)


def twice(dot_fn, x, w):
    rows = x.shape[0]
    both = dot_fn(jnp.concatenate(split(x), axis=0), w)
    return both[:rows] + both[rows:]


def packed(x):
    x = x.astype(BF16)
    return jnp.concatenate([x[:16], x[16:]], axis=1)


def where_is(index):
    return (index // 32, lax.rem(index, 32))


def partners(me):
    out = []
    for level in (2, 1, 0):
        members = 2**level
        cluster, member = me // members, lax.rem(me, members)
        first = (0, 4, 12)[level]
        for slot, offset in enumerate(OFFSETS):
            for c in range(members):
                to = (cluster - offset) * members + c
                out.append((level, to, first + slot * members + member, (cluster + offset) * members + c, first + slot * members + c))
    return out


def kernel(
    near_index, near_count, far_index,
    vectors_hbm, basis_hbm, near_hbm, couple_hbm, transfer_hbm, lcouple_hbm, ltransfer_hbm,
    out_ref,
    window, basis, blocks, couple, transfer, lcouple, ltransfer,
    coeffs, doubled, ups, arrived, weights,
    load_sem, vec_send, vec_recv, coef_send, coef_recv, up_send, up_recv,
):
    me = lax.axis_index("gx") * 32 + lax.axis_index("gy")

    def inside(device):
        return jnp.logical_and(device >= 0, device < NODES)

    loads = [
        pltpu.make_async_copy(source, target, load_sem.at[i])
        for i, (source, target) in enumerate((
            (vectors_hbm, window.at[pl.ds(8, 4)]),
            (basis_hbm, basis),
            (transfer_hbm, transfer),
            (ltransfer_hbm, ltransfer),
            (lcouple_hbm, lcouple),
            (couple_hbm, couple),
            (near_hbm, blocks),
        ))
    ]
    for load in loads:
        load.start()

    far = partners(me)
    barrier = pltpu.get_barrier_semaphore()
    greeted = [me + d for d in NEAR_OFFSETS] + [p[1] for p in far]
    expected = jnp.int32(0)
    for device in greeted:
        there = inside(device)
        expected = expected + there.astype(jnp.int32)

        @pl.when(there)
        def _():
            pl.semaphore_signal(barrier, inc=1, device_id=where_is(device), device_id_type=MESH)

    for _, _, _, source, slot in far:
        @pl.when(jnp.logical_not(inside(source)))
        def _():
            arrived[slot] = jnp.zeros((16, 128), BF16)

    pl.semaphore_wait(barrier, expected)

    def vec_copy(i, d):
        return pltpu.make_async_remote_copy(
            src_ref=vectors_hbm, dst_ref=window.at[pl.ds((2 - d) * 4, 4)],
            send_sem=vec_send.at[i], recv_sem=vec_recv.at[3 - i],
            device_id=where_is(me + d), device_id_type=MESH)

    def coef_copy(i, d):
        return pltpu.make_async_remote_copy(
            src_ref=coeffs.at[2], dst_ref=coeffs.at[2 - d],
            send_sem=coef_send.at[i], recv_sem=coef_recv.at[3 - i],
            device_id=where_is(me + d), device_id_type=MESH)

    def up_copy(i):
        level, to, slot, _, _ = far[i]
        return pltpu.make_async_remote_copy(
            src_ref=ups.at[level], dst_ref=arrived.at[slot],
            send_sem=up_send.at[i], recv_sem=up_recv.at[slot],
            device_id=where_is(to), device_id_type=MESH)

    for i, d in enumerate(NEAR_OFFSETS):
        pl.when(inside(me + d))(vec_copy(i, d).start)

    for load in loads[:4]:
        load.wait()
    own = [dot(window[8 + t], basis[t]).astype(BF16) for t in range(4)]
    coefficients = jnp.concatenate(own, axis=1)
    coeffs[2] = coefficients
    up0 = dot(coefficients, transfer[...].reshape(256, 64))
    up1 = twice(dot, up0, ltransfer[0, 0])
    up2 = twice(dot, up1, ltransfer[1, 0])
    ups[0] = packed(up0)
    ups[1] = packed(up1)
    ups[2] = packed(up2)
    for i, p in enumerate(far):
        pl.when(inside(p[1]))(up_copy(i).start)
    for i, d in enumerate(NEAR_OFFSETS):
        pl.when(inside(me + d))(coef_copy(i, d).start)

    loads[4].wait()
    transfer_all = transfer[...].reshape(256, 64)
    step = lcouple[0, 0].reshape(256, 64)
    mats = [step.astype(F32)]
    mats.append(dot_t(lcouple[1, 0].reshape(256, 64), ltransfer[0, 0]))
    mats.append(twice(dot_t, dot_t(lcouple[2, 0].reshape(256, 64), ltransfer[1, 0]), ltransfer[0, 0]))
    for level in range(3):
        high, low = split(twice(dot_t, mats[level], transfer_all))
        weights[0, level] = high
        weights[1, level] = low

    lane = lax.broadcasted_iota(jnp.int32, (32, 128), 1)
    left = lane < 64
    left16 = left[:16]

    def level_part(level):
        members = 2**level
        first = (0, 4, 12)[level]
        sums = []
        for slot in range(4):
            total = arrived[first + slot * members].astype(F32)
            for c in range(1, members):
                total = total + arrived[first + slot * members + c].astype(F32)
            sums.append(total)
        parts = []
        for a, b in ((0, 1), (2, 3)):
            top = jnp.where(left16, sums[a], pltpu.roll(sums[b], 64, 1))
            low = jnp.where(left16, pltpu.roll(sums[a], 64, 1), sums[b])
            parts.append(jnp.concatenate([top, low], axis=0))
        high, low = split(jnp.concatenate(parts, axis=1))
        both = dot(jnp.concatenate([high, low], axis=0), weights[0, level])
        return both[:32] + both[32:] + dot(high, weights[1, level])

    def wait_level(level):
        first, count = ((0, 4), (4, 8), (12, 16))[level]
        for i, (_, _, _, source, slot) in enumerate(far):
            if first <= slot_of[i] < first + count:
                pl.when(inside(source))(
                    pltpu.make_async_remote_copy(
                        src_ref=ups.at[level], dst_ref=arrived.at[slot],
                        send_sem=up_send.at[i], recv_sem=up_recv.at[slot],
                        device_id=where_is(source), device_id_type=MESH).wait_recv)

    slot_of = [p[4] for p in far]

    for i, d in enumerate(NEAR_OFFSETS):
        pl.when(inside(me - d))(coef_copy(i, d).wait_recv)

    loads[5].wait()
    for block in range(5):
        for pair in range(2):
            two = coeffs[block, :, pl.ds(pair * 128, 128)].astype(F32)
            turned = pltpu.roll(two, 64, 1)
            doubled[block * 4 + pair * 2] = jnp.where(left, two, turned).astype(BF16)
            doubled[block * 4 + pair * 2 + 1] = jnp.where(left, turned, two).astype(BF16)
    base = (me - 2) * 4

    def place(leaf):
        return jnp.clip(leaf - base, 0, 19)

    local = []
    for t in range(4):
        cols = []
        for j in range(0, 6, 2):
            first = doubled[place(far_index[t, j])]
            second = doubled[place(far_index[t, j + 1])]
            cols.append(jnp.where(left, first, second))
        local.append(dot(jnp.concatenate(cols, axis=1), couple[t].reshape(384, 64)))
    field = jnp.concatenate(local, axis=1)

    wait_level(0)
    field = field + level_part(0)

    loads[6].wait()
    for i, d in enumerate(NEAR_OFFSETS):
        pl.when(inside(me - d))(vec_copy(i, d).wait_recv)
    for t in range(4):
        picked = []
        for j in range(3):
            rows = window[place(near_index[t, j])]
            picked.append(jnp.where(j < near_count[t], rows, jnp.zeros_like(rows)))
        out_ref[t] = dot(jnp.concatenate(picked, axis=1), blocks[t].reshape(768, 256))

    wait_level(1)
    field = field + level_part(1)
    for i, d in enumerate(NEAR_OFFSETS):
        pl.when(inside(me + d))(vec_copy(i, d).wait_send)
        pl.when(inside(me + d))(coef_copy(i, d).wait_send)
    for i, p in enumerate(far):
        pl.when(inside(p[1]))(up_copy(i).wait_send)
    wait_level(2)
    field = (field + level_part(2)).astype(BF16)
    for t in range(4):
        out_ref[t] = out_ref[t] + dot_t(field[:, t * 64:(t + 1) * 64], basis[t])


def on_device(vectors, leaf_basis, near_blocks, near_index, near_count, leaf_couple, far_index, leaf_transfer, level_couple, level_transfer):
    smem = pl.BlockSpec(memory_space=pltpu.SMEM)
    hbm = pl.BlockSpec(memory_space=pltpu.HBM)
    dma = pltpu.SemaphoreType.DMA
    return pl.pallas_call(
        kernel,
        out_shape=jax.ShapeDtypeStruct((4, 32, 256), F32),
        in_specs=[smem] * 3 + [hbm] * 7,
        out_specs=pl.BlockSpec(memory_space=pltpu.VMEM),
        scratch_shapes=[
            pltpu.VMEM((20, 32, 256), BF16),
            pltpu.VMEM((4, 256, 64), BF16),
            pltpu.VMEM((4, 3, 256, 256), BF16),
            pltpu.VMEM((4, 6, 64, 64), BF16),
            pltpu.VMEM((4, 64, 64), BF16),
            pltpu.VMEM((3, 1, 4, 64, 64), BF16),
            pltpu.VMEM((2, 1, 64, 64), BF16),
            pltpu.VMEM((5, 32, 256), BF16),
            pltpu.VMEM((20, 32, 128), BF16),
            pltpu.VMEM((3, 16, 128), BF16),
            pltpu.VMEM((28, 16, 128), BF16),
            pltpu.VMEM((2, 3, 256, 256), BF16),
            dma((7,)), dma((4,)), dma((4,)), dma((4,)), dma((4,)), dma((28,)), dma((28,)),
        ],
        compiler_params=pltpu.CompilerParams(
            collective_id=0, has_side_effects=True, vmem_limit_bytes=32 * 2**20),
        name="h2_product",
    )(near_index, near_count, far_index, vectors, leaf_basis, near_blocks, leaf_couple, leaf_transfer, level_couple, level_transfer)


def solution(mesh):
    dim = P(("gx", "gy"))
    in_specs = (dim, dim, dim, dim, dim, dim, dim, dim, P(None, ("gx", "gy")), P(None, ("gx", "gy")))
    return jax.shard_map(on_device, mesh=mesh, in_specs=in_specs, out_specs=dim, check_vma=False)
```

time: 163 us -> 30.8 us (0.19)
  the two profiles are of different devices: /device:TPU:256 before, /device:TPU:9 now
where the time goes in v1:
time: 30.8 us; the launch traced here: 30.4 us
  Pallas kernels  20.8 us (68%)
  local copies, waits for them, and re-layouts  9.51 us (31%)
    pallas_call x1, Pallas kernels, on_device(): pl.pallas_call(kernel, out_shape=jax.ShapeDtypeStruct((4, 32, 256), F32),...  20.8 us
    unnamed x20, local copies, waits for them, and re-layouts  9.51 us

profile of v1, /device:TPU:9, one launch (start us, length us, event | category | flops | bytes accessed | tf_op | source)
XLA Modules:
  0.0 30.4 jit_solution(11067541921699694336)
XLA Ops:
  0.0 1.1 %copy.11.basis_hbm = bf16[4,256,64]{2,1,0:T(8,128)(2,1)S(1)} copy(bf16[4,256,64]{1,2,0:T(8,128)(2,1)} %param.11) | data formatting | bytes 262144 | tf_op args[1]
  1.1 0.0 copy-start
  1.1 1.4 %copy-done = bf16[4,3,256,256]{3,2,1,0:T(8,128)(2,1)S(1)} copy-done((bf16[4,3,256,256]{3,2,1,0:T(8,128)(2,1)S(1)}, bf16[4,3,256,256]{3,2,1,0:T(8,128)(2,1)}, u32[]{:S(2)}) %copy-start) | copy-done | bytes 1572888
  2.5 0.0 copy-start.1
  2.5 1.0 %copy-done.1 = bf16[4,6,64,64]{3,2,1,0:T(8,128)(2,1)S(1)} copy-done((bf16[4,6,64,64]{3,2,1,0:T(8,128)(2,1)S(1)}, bf16[4,6,64,64]{3,2,1,0:T(8,128)(2,1)}, u32[]{:S(2)}) %copy-start.1) | copy-done | bytes 196632
  3.5 0.0 copy-start.2
  3.5 0.9 %copy-done.2 = bf16[3,1,4,64,64]{4,3,2,1,0:T(8,128)(2,1)S(1)} copy-done((bf16[3,1,4,64,64]{4,3,2,1,0:T(8,128)(2,1)S(1)}, bf16[3,1,4,64,64]{4,3,2,1,0:T(8,128)(2,1)}, u32[]{:S(2)}) %copy-start.2) | copy-done | bytes 98328
  4.4 0.0 copy-start.3
  4.4 0.8 %copy-done.3 = bf16[4,32,256]{2,1,0:T(8,128)(2,1)S(1)} copy-done((bf16[4,32,256]{2,1,0:T(8,128)(2,1)S(1)}, bf16[4,32,256]{2,1,0:T(8,128)(2,1)}, u32[]{:S(2)}) %copy-start.3) | copy-done | bytes 65560
  5.3 0.0 copy-start.4
  5.3 0.8 %copy-done.4 = bf16[4,64,64]{2,1,0:T(8,128)(2,1)S(1)} copy-done((bf16[4,64,64]{2,1,0:T(8,128)(2,1)S(1)}, bf16[4,64,64]{2,1,0:T(8,128)(2,1)}, u32[]{:S(2)}) %copy-start.4) | copy-done | bytes 32792
  6.1 0.0 copy-start.5
  6.1 0.8 %copy-done.5 = bf16[2,1,64,64]{3,2,1,0:T(8,128)(2,1)S(1)} copy-done((bf16[2,1,64,64]{3,2,1,0:T(8,128)(2,1)S(1)}, bf16[2,1,64,64]{3,2,1,0:T(8,128)(2,1)}, u32[]{:S(2)}) %copy-start.5) | copy-done | bytes 16408
  6.9 0.0 copy-start.6
  6.9 0.7 %copy-done.6 = s32[4,3]{1,0:T(4,128)S(1)} copy-done((s32[4,3]{1,0:T(4,128)S(1)}, s32[4,3]{1,0:T(4,128)}, u32[]{:S(2)}) %copy-start.6) | copy-done | bytes 72
  7.5 0.0 copy-start.7
  7.5 0.7 %copy-done.7 = s32[4,6]{1,0:T(4,128)S(1)} copy-done((s32[4,6]{1,0:T(4,128)S(1)}, s32[4,6]{1,0:T(4,128)}, u32[]{:S(2)}) %copy-start.7) | copy-done | bytes 120
  8.2 0.0 copy-start.8
  8.2 0.7 %copy-done.8 = s32[4]{0:T(128)S(1)} copy-done((s32[4]{0:T(128)S(1)}, s32[4]{0:T(128)}, u32[]{:S(2)}) %copy-start.8) | copy-done | bytes 40
  8.9 20.8 %h2_product.1 = f32[4,32,256]{2,1,0:T(8,128)S(1)} custom-call(s32[4,3]{1,0:T(4,128)S(1)} %copy-done.6, s32[4]{0:T(128)S(1)} %copy-done.8, s32[4,6]{1,0:T(4,128)S(1)} %copy-done.7, bf16[4,32,256]{2,1,0:T(8,128)(2,1)S(1)} %copy-done.3, bf16[4,256,64]{2,1,0:T(8,128)(2,1)S(1)} %copy.11.basis_hbm, bf16[4,3,256,256]{3,2,1,0:T(8,128)(2,1)S(1)} %copy-done, ...), custom_call_target="tpu_custom_call" | custom-call | tf_op jit(solution)/shard_map/h2_product/pallas_call | solution.py:241
  29.7 0.7 %copy.13 = f32[4,32,256]{2,1,0:T(8,128)} copy(f32[4,32,256]{2,1,0:T(8,128)S(1)} %h2_product.1) | data formatting | bytes 262144
Async XLA Ops:
  1.1 1.4 %copy-start = (bf16[4,3,256,256]{3,2,1,0:T(8,128)(2,1)S(1)}, bf16[4,3,256,256]{3,2,1,0:T(8,128)(2,1)}, u32[]{:S(2)}) copy-start(bf16[4,3,256,256]{3,2,1,0:T(8,128)(2,1)} %near_hbm.1) | copy-start | bytes 4718596
  2.5 1.0 %copy-start.1 = (bf16[4,6,64,64]{3,2,1,0:T(8,128)(2,1)S(1)}, bf16[4,6,64,64]{3,2,1,0:T(8,128)(2,1)}, u32[]{:S(2)}) copy-start(bf16[4,6,64,64]{3,2,1,0:T(8,128)(2,1)} %couple_hbm.1) | copy-start | bytes 589828
  3.5 0.9 %copy-start.2 = (bf16[3,1,4,64,64]{4,3,2,1,0:T(8,128)(2,1)S(1)}, bf16[3,1,4,64,64]{4,3,2,1,0:T(8,128)(2,1)}, u32[]{:S(2)}) copy-start(bf16[3,1,4,64,64]{4,3,2,1,0:T(8,128)(2,1)} %lcouple_hbm.1) | copy-start | bytes 294916
  4.4 0.8 %copy-start.3 = (bf16[4,32,256]{2,1,0:T(8,128)(2,1)S(1)}, bf16[4,32,256]{2,1,0:T(8,128)(2,1)}, u32[]{:S(2)}) copy-start(bf16[4,32,256]{2,1,0:T(8,128)(2,1)} %vectors_hbm.1) | copy-start | bytes 196612
  5.3 0.8 %copy-start.4 = (bf16[4,64,64]{2,1,0:T(8,128)(2,1)S(1)}, bf16[4,64,64]{2,1,0:T(8,128)(2,1)}, u32[]{:S(2)}) copy-start(bf16[4,64,64]{2,1,0:T(8,128)(2,1)} %transfer_hbm.1) | copy-start | bytes 98308
  6.1 0.8 %copy-start.5 = (bf16[2,1,64,64]{3,2,1,0:T(8,128)(2,1)S(1)}, bf16[2,1,64,64]{3,2,1,0:T(8,128)(2,1)}, u32[]{:S(2)}) copy-start(bf16[2,1,64,64]{3,2,1,0:T(8,128)(2,1)} %ltransfer_hbm.1) | copy-start | bytes 49156
  6.9 0.7 %copy-start.6 = (s32[4,3]{1,0:T(4,128)S(1)}, s32[4,3]{1,0:T(4,128)}, u32[]{:S(2)}) copy-start(s32[4,3]{1,0:T(4,128)} %near_index.1) | copy-start | bytes 148
  7.5 0.7 %copy-start.7 = (s32[4,6]{1,0:T(4,128)S(1)}, s32[4,6]{1,0:T(4,128)}, u32[]{:S(2)}) copy-start(s32[4,6]{1,0:T(4,128)} %far_index.1) | copy-start | bytes 292
  8.2 0.7 %copy-start.8 = (s32[4]{0:T(128)S(1)}, s32[4]{0:T(128)}, u32[]{:S(2)}) copy-start(s32[4]{0:T(128)} %near_count.1) | copy-start | bytes 52

commit v2 on v1

--- a/solution.py
+++ b/solution.py
@@ -54,11 +54,11 @@
 
 
 def kernel(
-    near_index, near_count, far_index,
+    near_index_hbm, near_count_hbm, far_index_hbm,
     vectors_hbm, basis_hbm, near_hbm, couple_hbm, transfer_hbm, lcouple_hbm, ltransfer_hbm,
     out_ref,
     window, basis, blocks, couple, transfer, lcouple, ltransfer,
-    coeffs, doubled, ups, arrived, weights,
+    coeffs, doubled, ups, arrived, weights, near_index, near_count, far_index,
     load_sem, vec_send, vec_recv, coef_send, coef_recv, up_send, up_recv,
 ):
     me = lax.axis_index("gx") * 32 + lax.axis_index("gy")
@@ -76,6 +76,9 @@
             (lcouple_hbm, lcouple),
             (couple_hbm, couple),
             (near_hbm, blocks),
+            (near_index_hbm, near_index),
+            (near_count_hbm, near_count),
+            (far_index_hbm, far_index),
         ))
     ]
     for load in loads:
@@ -124,7 +127,7 @@
 
     for load in loads[:4]:
         load.wait()
-    own = [dot(window[8 + t], basis[t]).astype(BF16) for t in range(4)]
+    own = [dot_t(window[8 + t], basis[t]).astype(BF16) for t in range(4)]
     coefficients = jnp.concatenate(own, axis=1)
     coeffs[2] = coefficients
     up0 = dot(coefficients, transfer[...].reshape(256, 64))
@@ -187,6 +190,7 @@
         pl.when(inside(me - d))(coef_copy(i, d).wait_recv)
 
     loads[5].wait()
+    loads[9].wait()
     for block in range(5):
         for pair in range(2):
             two = coeffs[block, :, pl.ds(pair * 128, 128)].astype(F32)
@@ -212,6 +216,8 @@
     field = field + level_part(0)
 
     loads[6].wait()
+    loads[7].wait()
+    loads[8].wait()
     for i, d in enumerate(NEAR_OFFSETS):
         pl.when(inside(me - d))(vec_copy(i, d).wait_recv)
     for t in range(4):
@@ -231,21 +237,20 @@
     wait_level(2)
     field = (field + level_part(2)).astype(BF16)
     for t in range(4):
-        out_ref[t] = out_ref[t] + dot_t(field[:, t * 64:(t + 1) * 64], basis[t])
+        out_ref[t] = out_ref[t] + dot(field[:, t * 64:(t + 1) * 64], basis[t])
 
 
 def on_device(vectors, leaf_basis, near_blocks, near_index, near_count, leaf_couple, far_index, leaf_transfer, level_couple, level_transfer):
-    smem = pl.BlockSpec(memory_space=pltpu.SMEM)
     hbm = pl.BlockSpec(memory_space=pltpu.HBM)
     dma = pltpu.SemaphoreType.DMA
     return pl.pallas_call(
         kernel,
         out_shape=jax.ShapeDtypeStruct((4, 32, 256), F32),
-        in_specs=[smem] * 3 + [hbm] * 7,
+        in_specs=[hbm] * 10,
         out_specs=pl.BlockSpec(memory_space=pltpu.VMEM),
         scratch_shapes=[
             pltpu.VMEM((20, 32, 256), BF16),
-            pltpu.VMEM((4, 256, 64), BF16),
+            pltpu.VMEM((4, 64, 256), BF16),
             pltpu.VMEM((4, 3, 256, 256), BF16),
             pltpu.VMEM((4, 6, 64, 64), BF16),
             pltpu.VMEM((4, 64, 64), BF16),
@@ -256,12 +261,15 @@
             pltpu.VMEM((3, 16, 128), BF16),
             pltpu.VMEM((28, 16, 128), BF16),
             pltpu.VMEM((2, 3, 256, 256), BF16),
-            dma((7,)), dma((4,)), dma((4,)), dma((4,)), dma((4,)), dma((28,)), dma((28,)),
+            pltpu.SMEM((4, 3), jnp.int32),
+            pltpu.SMEM((4,), jnp.int32),
+            pltpu.SMEM((4, 6), jnp.int32),
+            dma((10,)), dma((4,)), dma((4,)), dma((4,)), dma((4,)), dma((28,)), dma((28,)),
         ],
         compiler_params=pltpu.CompilerParams(
             collective_id=0, has_side_effects=True, vmem_limit_bytes=32 * 2**20),
         name="h2_product",
-    )(near_index, near_count, far_index, vectors, leaf_basis, near_blocks, leaf_couple, leaf_transfer, level_couple, level_transfer)
+    )(*(pltpu.with_memory_space_constraint(x, pltpu.HBM) for x in (near_index, near_count, far_index, vectors, jnp.swapaxes(leaf_basis, 1, 2), near_blocks, leaf_couple, leaf_transfer, level_couple, level_transfer)))
 
 
 def solution(mesh):

time: 30.8 us -> 20.5 us (0.67)
  local copies, waits for them, and re-layouts: 9.51 us -> 0.66 us
  Pallas kernels: 20.8 us -> 19.7 us
    unnamed x20 -> x1, local copies, waits for them, and re-layouts: 9.51 us -> 0.66 us
    pallas_call x1, Pallas kernels: 20.8 us -> 19.7 us  [on_device(): pl.pallas_call(kernel, out_shape=jax.ShapeDtypeStruct((4, 32, 256), F32),...]
where the time goes in v2:
time: 20.5 us; the launch traced here: 20.4 us
  Pallas kernels  19.7 us (96%)
  local copies, waits for them, and re-layouts  0.66 us (3%)
    pallas_call x1, Pallas kernels, on_device(): pl.pallas_call(kernel, out_shape=jax.ShapeDtypeStruct((4, 32, 256), F32),...  19.7 us
    unnamed x1, local copies, waits for them, and re-layouts  0.66 us

profile of v2, /device:TPU:9, one launch (start us, length us, event | category | flops | bytes accessed | tf_op | source)
XLA Modules:
  0.0 20.4 jit_solution(17947709894431256068)
XLA Ops:
  0.0 19.7 %h2_product.1 = f32[4,32,256]{2,1,0:T(8,128)S(1)} custom-call(s32[4,3]{1,0:T(4,128)} %near_index_hbm.1, s32[4]{0:T(128)} %near_count_hbm.1, s32[4,6]{1,0:T(4,128)} %far_index_hbm.1, bf16[4,32,256]{2,1,0:T(8,128)(2,1)} %vectors_hbm.1, bf16[4,64,256]{2,1,0:T(8,128)(2,1)} %bitcast.1, bf16[4,3,256,256]{3,2,1,0:T(8,128)(2,1)} %near_hbm.1, ...), custom_call_target="tpu_custom_call" | custom-call | tf_op jit(solution)/shard_map/h2_product/pallas_call | solution.py:246
  19.7 0.7 %copy.12 = f32[4,32,256]{2,1,0:T(8,128)} copy(f32[4,32,256]{2,1,0:T(8,128)S(1)} %h2_product.1) | data formatting | bytes 262144

commit v3 on v2

--- a/solution.py
+++ b/solution.py
@@ -37,20 +37,14 @@
 
 
 def where_is(index):
-    return (index // 32, lax.rem(index, 32))
-
-
-def partners(me):
-    out = []
-    for level in (2, 1, 0):
-        members = 2**level
-        cluster, member = me // members, lax.rem(me, members)
-        first = (0, 4, 12)[level]
-        for slot, offset in enumerate(OFFSETS):
-            for c in range(members):
-                to = (cluster - offset) * members + c
-                out.append((level, to, first + slot * members + member, (cluster + offset) * members + c, first + slot * members + c))
-    return out
+    return (jnp.right_shift(index, 5), jnp.bitwise_and(index, 31))
+
+
+FIRST = (0, 4, 12)
+
+
+def both(a, b):
+    return jnp.logical_and(a, b)
 
 
 def kernel(
@@ -59,7 +53,7 @@
     out_ref,
     window, basis, blocks, couple, transfer, lcouple, ltransfer,
     coeffs, doubled, ups, arrived, weights, near_index, near_count, far_index,
-    load_sem, vec_send, vec_recv, coef_send, coef_recv, up_send, up_recv,
+    load_sem, vec_send, vec_recv, coef_send, coef_recv, up_send, up_recv, known,
 ):
     me = lax.axis_index("gx") * 32 + lax.axis_index("gy")
 
@@ -84,24 +78,32 @@
     for load in loads:
         load.start()
 
-    far = partners(me)
     barrier = pltpu.get_barrier_semaphore()
-    greeted = [me + d for d in NEAR_OFFSETS] + [p[1] for p in far]
-    expected = jnp.int32(0)
-    for device in greeted:
-        there = inside(device)
-        expected = expected + there.astype(jnp.int32)
-
-        @pl.when(there)
-        def _():
-            pl.semaphore_signal(barrier, inc=1, device_id=where_is(device), device_id_type=MESH)
-
-    for _, _, _, source, slot in far:
-        @pl.when(jnp.logical_not(inside(source)))
-        def _():
-            arrived[slot] = jnp.zeros((16, 128), BF16)
-
-    pl.semaphore_wait(barrier, expected)
+
+    def tell(semaphore, distances):
+        count = jnp.int32(0)
+        for d in distances:
+            there = inside(me + d)
+            count = count + there.astype(jnp.int32)
+
+            @pl.when(there)
+            def _():
+                pl.semaphore_signal(semaphore, inc=1, device_id=where_is(me + d), device_id_type=MESH)
+
+        return count
+
+    beside = tell(barrier, (-4, 4, -3, 3, -2, 2, -1, 1))
+
+    for level in range(3):
+        members = 2**level
+        cluster = jnp.right_shift(me, level)
+        for slot, offset in enumerate(OFFSETS):
+            source = cluster + offset
+
+            @pl.when(jnp.logical_or(source < 0, source >= NODES // members))
+            def _():
+                for c in range(members):
+                    arrived[FIRST[level] + slot * members + c] = jnp.zeros((16, 128), BF16)
 
     def vec_copy(i, d):
         return pltpu.make_async_remote_copy(
@@ -115,15 +117,34 @@
             send_sem=coef_send.at[i], recv_sem=coef_recv.at[3 - i],
             device_id=where_is(me + d), device_id_type=MESH)
 
-    def up_copy(i):
-        level, to, slot, _, _ = far[i]
+    def up_copy(level, slot, c):
+        members = 2**level
+        first = FIRST[level] + slot * members
         return pltpu.make_async_remote_copy(
-            src_ref=ups.at[level], dst_ref=arrived.at[slot],
-            send_sem=up_send.at[i], recv_sem=up_recv.at[slot],
-            device_id=where_is(to), device_id_type=MESH)
-
-    for i, d in enumerate(NEAR_OFFSETS):
-        pl.when(inside(me + d))(vec_copy(i, d).start)
+            src_ref=ups.at[level], dst_ref=arrived.at[first + jnp.bitwise_and(me, members - 1)],
+            send_sem=up_send.at[first + c], recv_sem=up_recv.at[first + jnp.bitwise_and(me, members - 1)],
+            device_id=where_is((jnp.right_shift(me, level) - OFFSETS[slot]) * members + c), device_id_type=MESH)
+
+    def arrival(level, slot, c):
+        place = FIRST[level] + slot * 2**level + c
+        return pltpu.make_async_remote_copy(
+            src_ref=ups.at[level], dst_ref=arrived.at[place],
+            send_sem=up_send.at[place], recv_sem=up_recv.at[place],
+            device_id=where_is(jnp.bitwise_and(me + 1, NODES - 1)), device_id_type=MESH)
+
+    def goes(level, slot):
+        to = jnp.right_shift(me, level) - OFFSETS[slot]
+        return both(to >= 0, to < NODES // 2**level)
+
+    def comes(level, slot):
+        source = jnp.right_shift(me, level) + OFFSETS[slot]
+        return both(source >= 0, source < NODES // 2**level)
+
+    def send_up(level, slot):
+        @pl.when(goes(level, slot))
+        def _():
+            for c in range(2**level):
+                up_copy(level, slot, c).start()
 
     for load in loads[:4]:
         load.wait()
@@ -136,10 +157,23 @@
     ups[0] = packed(up0)
     ups[1] = packed(up1)
     ups[2] = packed(up2)
-    for i, p in enumerate(far):
-        pl.when(inside(p[1]))(up_copy(i).start)
+
+    pl.semaphore_wait(barrier, beside)
+    relayed = tell(known.at[0], (-4, 4))
     for i, d in enumerate(NEAR_OFFSETS):
-        pl.when(inside(me + d))(coef_copy(i, d).start)
+        @pl.when(inside(me + d))
+        def _():
+            coef_copy(i, d).start()
+            vec_copy(i, d).start()
+    for slot in range(4):
+        send_up(0, slot)
+    pl.semaphore_wait(known.at[0], relayed)
+    relayed = tell(known.at[1], (-8, 8))
+    for slot in range(4):
+        send_up(1, slot)
+    pl.semaphore_wait(known.at[1], relayed)
+    for slot in (0, 3, 1, 2):
+        send_up(2, slot)
 
     loads[4].wait()
     transfer_all = transfer[...].reshape(256, 64)
@@ -175,16 +209,11 @@
         return both[:32] + both[32:] + dot(high, weights[1, level])
 
     def wait_level(level):
-        first, count = ((0, 4), (4, 8), (12, 16))[level]
-        for i, (_, _, _, source, slot) in enumerate(far):
-            if first <= slot_of[i] < first + count:
-                pl.when(inside(source))(
-                    pltpu.make_async_remote_copy(
-                        src_ref=ups.at[level], dst_ref=arrived.at[slot],
-                        send_sem=up_send.at[i], recv_sem=up_recv.at[slot],
-                        device_id=where_is(source), device_id_type=MESH).wait_recv)
-
-    slot_of = [p[4] for p in far]
+        for slot in range(4):
+            @pl.when(comes(level, slot))
+            def _():
+                for c in range(2**level):
+                    arrival(level, slot, c).wait_recv()
 
     for i, d in enumerate(NEAR_OFFSETS):
         pl.when(inside(me - d))(coef_copy(i, d).wait_recv)
@@ -229,15 +258,22 @@
 
     wait_level(1)
     field = field + level_part(1)
-    for i, d in enumerate(NEAR_OFFSETS):
-        pl.when(inside(me + d))(vec_copy(i, d).wait_send)
-        pl.when(inside(me + d))(coef_copy(i, d).wait_send)
-    for i, p in enumerate(far):
-        pl.when(inside(p[1]))(up_copy(i).wait_send)
     wait_level(2)
     field = (field + level_part(2)).astype(BF16)
     for t in range(4):
         out_ref[t] = out_ref[t] + dot(field[:, t * 64:(t + 1) * 64], basis[t])
+
+    for i, d in enumerate(NEAR_OFFSETS):
+        @pl.when(inside(me + d))
+        def _():
+            vec_copy(i, d).wait_send()
+            coef_copy(i, d).wait_send()
+    for level in range(3):
+        for slot in range(4):
+            @pl.when(goes(level, slot))
+            def _():
+                for c in range(2**level):
+                    up_copy(level, slot, c).wait_send()
 
 
 def on_device(vectors, leaf_basis, near_blocks, near_index, near_count, leaf_couple, far_index, leaf_transfer, level_couple, level_transfer):
@@ -264,7 +300,7 @@
             pltpu.SMEM((4, 3), jnp.int32),
             pltpu.SMEM((4,), jnp.int32),
             pltpu.SMEM((4, 6), jnp.int32),
-            dma((10,)), dma((4,)), dma((4,)), dma((4,)), dma((4,)), dma((28,)), dma((28,)),
+            dma((10,)), dma((4,)), dma((4,)), dma((4,)), dma((4,)), dma((28,)), dma((28,)), pltpu.SemaphoreType.REGULAR((2,)),
         ],
         compiler_params=pltpu.CompilerParams(
             collective_id=0, has_side_effects=True, vmem_limit_bytes=32 * 2**20),

time: 20.5 us -> 19.7 us (0.961)
  the two profiles are of different devices: /device:TPU:9 before, /device:TPU:257 now
where the time goes in v3:
time: 19.7 us; the launch traced here: 19.6 us
  Pallas kernels  18.9 us (96%)
  local copies, waits for them, and re-layouts  0.66 us (3%)
    pallas_call x1, Pallas kernels, on_device(): pl.pallas_call(kernel, out_shape=jax.ShapeDtypeStruct((4, 32, 256), F32),...  18.9 us
    unnamed x1, local copies, waits for them, and re-layouts  0.66 us

profile of v3, /device:TPU:257, one launch (start us, length us, event | category | flops | bytes accessed | tf_op | source)
XLA Modules:
  0.0 19.6 jit_solution(4838742151513768023)
XLA Ops:
  0.0 18.9 %h2_product.1 = f32[4,32,256]{2,1,0:T(8,128)S(1)} custom-call(s32[4,3]{1,0:T(4,128)} %near_index_hbm.1, s32[4]{0:T(128)} %near_count_hbm.1, s32[4,6]{1,0:T(4,128)} %far_index_hbm.1, bf16[4,32,256]{2,1,0:T(8,128)(2,1)} %vectors_hbm.1, bf16[4,64,256]{2,1,0:T(8,128)(2,1)} %bitcast.1, bf16[4,3,256,256]{3,2,1,0:T(8,128)(2,1)} %near_hbm.1, ...), custom_call_target="tpu_custom_call" | custom-call | tf_op jit(solution)/shard_map/h2_product/pallas_call | solution.py:282
  19.0 0.7 %copy.12 = f32[4,32,256]{2,1,0:T(8,128)} copy(f32[4,32,256]{2,1,0:T(8,128)S(1)} %h2_product.1) | data formatting | bytes 262144

commit v4 on v3

--- a/solution.py
+++ b/solution.py
@@ -40,7 +40,8 @@
     return (jnp.right_shift(index, 5), jnp.bitwise_and(index, 31))
 
 
-FIRST = (0, 4, 12)
+FIRST = (0, 4, 8)
+CHIPS = (1, 1, 2)
 
 
 def both(a, b):
@@ -52,8 +53,8 @@
     vectors_hbm, basis_hbm, near_hbm, couple_hbm, transfer_hbm, lcouple_hbm, ltransfer_hbm,
     out_ref,
     window, basis, blocks, couple, transfer, lcouple, ltransfer,
-    coeffs, doubled, ups, arrived, weights, near_index, near_count, far_index,
-    load_sem, vec_send, vec_recv, coef_send, coef_recv, up_send, up_recv, known,
+    coeffs, doubled, ups, arrived, weights, halves, near_index, near_count, far_index,
+    load_sem, vec_send, vec_recv, coef_send, coef_recv, up_send, up_recv, swap_sem, known,
 ):
     me = lax.axis_index("gx") * 32 + lax.axis_index("gy")
 
@@ -92,7 +93,7 @@
 
         return count
 
-    beside = tell(barrier, (-4, 4, -3, 3, -2, 2, -1, 1))
+    beside = tell(barrier, (-8, 8, -6, 6, -4, 4, -3, 3, -2, 2, -1, 1))
 
     for level in range(3):
         members = 2**level
@@ -102,8 +103,8 @@
 
             @pl.when(jnp.logical_or(source < 0, source >= NODES // members))
             def _():
-                for c in range(members):
-                    arrived[FIRST[level] + slot * members + c] = jnp.zeros((16, 128), BF16)
+                for c in range(CHIPS[level]):
+                    arrived[FIRST[level] + slot * CHIPS[level] + c] = jnp.zeros((16, 128), BF16)
 
     def vec_copy(i, d):
         return pltpu.make_async_remote_copy(
@@ -117,21 +118,30 @@
             send_sem=coef_send.at[i], recv_sem=coef_recv.at[3 - i],
             device_id=where_is(me + d), device_id_type=MESH)
 
+    core, chip = jnp.bitwise_and(me, 1), jnp.bitwise_and(jnp.right_shift(me, 1), 1)
+
     def up_copy(level, slot, c):
-        members = 2**level
-        first = FIRST[level] + slot * members
+        first = FIRST[level] + slot * CHIPS[level]
+        if level == 2:
+            to, mine = (jnp.right_shift(me, 2) - OFFSETS[slot]) * 4 + 2 * c + core, first + chip
+        else:
+            to, mine = me - OFFSETS[slot] * 2**level, first
         return pltpu.make_async_remote_copy(
-            src_ref=ups.at[level], dst_ref=arrived.at[first + jnp.bitwise_and(me, members - 1)],
-            send_sem=up_send.at[first + c], recv_sem=up_recv.at[first + jnp.bitwise_and(me, members - 1)],
-            device_id=where_is((jnp.right_shift(me, level) - OFFSETS[slot]) * members + c), device_id_type=MESH)
+            src_ref=ups.at[level], dst_ref=arrived.at[mine],
+            send_sem=up_send.at[first + c], recv_sem=up_recv.at[mine],
+            device_id=where_is(to), device_id_type=MESH)
 
     def arrival(level, slot, c):
-        place = FIRST[level] + slot * 2**level + c
+        place = FIRST[level] + slot * CHIPS[level] + c
         return pltpu.make_async_remote_copy(
             src_ref=ups.at[level], dst_ref=arrived.at[place],
             send_sem=up_send.at[place], recv_sem=up_recv.at[place],
             device_id=where_is(jnp.bitwise_and(me + 1, NODES - 1)), device_id_type=MESH)
 
+    swap = pltpu.make_async_remote_copy(
+        src_ref=halves.at[0], dst_ref=halves.at[1], send_sem=swap_sem.at[0], recv_sem=swap_sem.at[1],
+        device_id=where_is(jnp.bitwise_xor(me, 1)), device_id_type=MESH)
+
     def goes(level, slot):
         to = jnp.right_shift(me, level) - OFFSETS[slot]
         return both(to >= 0, to < NODES // 2**level)
@@ -143,7 +153,7 @@
     def send_up(level, slot):
         @pl.when(goes(level, slot))
         def _():
-            for c in range(2**level):
+            for c in range(CHIPS[level]):
                 up_copy(level, slot, c).start()
 
     for load in loads[:4]:
@@ -153,13 +163,15 @@
     coeffs[2] = coefficients
     up0 = dot(coefficients, transfer[...].reshape(256, 64))
     up1 = twice(dot, up0, ltransfer[0, 0])
-    up2 = twice(dot, up1, ltransfer[1, 0])
     ups[0] = packed(up0)
-    ups[1] = packed(up1)
-    ups[2] = packed(up2)
+    half = jnp.concatenate([up1[:16], up1[16:]], axis=1)
+    high, low = split(half)
+    halves[0, 0] = high
+    halves[0, 1] = low
 
     pl.semaphore_wait(barrier, beside)
-    relayed = tell(known.at[0], (-4, 4))
+    relayed = tell(known.at[0], (-8, 8))
+    swap.start()
     for i, d in enumerate(NEAR_OFFSETS):
         @pl.when(inside(me + d))
         def _():
@@ -167,11 +179,15 @@
             vec_copy(i, d).start()
     for slot in range(4):
         send_up(0, slot)
-    pl.semaphore_wait(known.at[0], relayed)
-    relayed = tell(known.at[1], (-8, 8))
+    swap.wait_recv()
+    half = half + (halves[1, 0].astype(F32) + halves[1, 1].astype(F32))
+    ups[1] = half.astype(BF16)
+    turned = pltpu.roll(half, 64, 1)
+    pair = jnp.concatenate([half, turned], axis=0)[:, :64]
+    ups[2] = packed(twice(dot, pair, ltransfer[1, 0]))
     for slot in range(4):
         send_up(1, slot)
-    pl.semaphore_wait(known.at[1], relayed)
+    pl.semaphore_wait(known.at[0], relayed)
     for slot in (0, 3, 1, 2):
         send_up(2, slot)
 
@@ -191,13 +207,12 @@
     left16 = left[:16]
 
     def level_part(level):
-        members = 2**level
-        first = (0, 4, 12)[level]
         sums = []
         for slot in range(4):
-            total = arrived[first + slot * members].astype(F32)
-            for c in range(1, members):
-                total = total + arrived[first + slot * members + c].astype(F32)
+            place = FIRST[level] + slot * CHIPS[level]
+            total = arrived[place].astype(F32)
+            for c in range(1, CHIPS[level]):
+                total = total + arrived[place + c].astype(F32)
             sums.append(total)
         parts = []
         for a, b in ((0, 1), (2, 3)):
@@ -212,7 +227,7 @@
         for slot in range(4):
             @pl.when(comes(level, slot))
             def _():
-                for c in range(2**level):
+                for c in range(CHIPS[level]):
                     arrival(level, slot, c).wait_recv()
 
     for i, d in enumerate(NEAR_OFFSETS):
@@ -263,6 +278,7 @@
     for t in range(4):
         out_ref[t] = out_ref[t] + dot(field[:, t * 64:(t + 1) * 64], basis[t])
 
+    swap.wait_send()
     for i, d in enumerate(NEAR_OFFSETS):
         @pl.when(inside(me + d))
         def _():
@@ -272,7 +288,7 @@
         for slot in range(4):
             @pl.when(goes(level, slot))
             def _():
-                for c in range(2**level):
+                for c in range(CHIPS[level]):
                     up_copy(level, slot, c).wait_send()
 
 
@@ -295,12 +311,13 @@
             pltpu.VMEM((5, 32, 256), BF16),
             pltpu.VMEM((20, 32, 128), BF16),
             pltpu.VMEM((3, 16, 128), BF16),
-            pltpu.VMEM((28, 16, 128), BF16),
+            pltpu.VMEM((16, 16, 128), BF16),
             pltpu.VMEM((2, 3, 256, 256), BF16),
+            pltpu.VMEM((2, 2, 16, 128), BF16),
             pltpu.SMEM((4, 3), jnp.int32),
             pltpu.SMEM((4,), jnp.int32),
             pltpu.SMEM((4, 6), jnp.int32),
-            dma((10,)), dma((4,)), dma((4,)), dma((4,)), dma((4,)), dma((28,)), dma((28,)), pltpu.SemaphoreType.REGULAR((2,)),
+            dma((10,)), dma((4,)), dma((4,)), dma((4,)), dma((4,)), dma((16,)), dma((16,)), dma((2,)), pltpu.SemaphoreType.REGULAR((1,)),
         ],
         compiler_params=pltpu.CompilerParams(
             collective_id=0, has_side_effects=True, vmem_limit_bytes=32 * 2**20),

time: 19.7 us -> 17.9 us (0.909)
  the two profiles are of different devices: /device:TPU:257 before, /device:TPU:9 now
where the time goes in v4:
time: 17.9 us; the launch traced here: 17.6 us
  Pallas kernels  16.9 us (94%)
  local copies, waits for them, and re-layouts  0.66 us (4%)
    pallas_call x1, Pallas kernels, on_device(): pl.pallas_call(kernel, out_shape=jax.ShapeDtypeStruct((4, 32, 256), F32),...  16.9 us
    unnamed x1, local copies, waits for them, and re-layouts  0.66 us

profile of v4, /device:TPU:9, one launch (start us, length us, event | category | flops | bytes accessed | tf_op | source)
XLA Modules:
  0.0 17.6 jit_solution(8488978887817930424)
XLA Ops:
  0.0 16.9 %h2_product.1 = f32[4,32,256]{2,1,0:T(8,128)S(1)} custom-call(s32[4,3]{1,0:T(4,128)} %near_index_hbm.1, s32[4]{0:T(128)} %near_count_hbm.1, s32[4,6]{1,0:T(4,128)} %far_index_hbm.1, bf16[4,32,256]{2,1,0:T(8,128)(2,1)} %vectors_hbm.1, bf16[4,64,256]{2,1,0:T(8,128)(2,1)} %bitcast.1, bf16[4,3,256,256]{3,2,1,0:T(8,128)(2,1)} %near_hbm.1, ...), custom_call_target="tpu_custom_call" | custom-call | tf_op jit(solution)/shard_map/h2_product/pallas_call | solution.py:298
  16.9 0.7 %copy.12 = f32[4,32,256]{2,1,0:T(8,128)} copy(f32[4,32,256]{2,1,0:T(8,128)S(1)} %h2_product.1) | data formatting | bytes 262144

commit v5 on v4

--- a/solution.py
+++ b/solution.py
@@ -76,7 +76,7 @@
             (far_index_hbm, far_index),
         ))
     ]
-    for load in loads:
+    for load in loads[:4]:
         load.start()
 
     barrier = pltpu.get_barrier_semaphore()
@@ -106,11 +106,19 @@
                 for c in range(CHIPS[level]):
                     arrived[FIRST[level] + slot * CHIPS[level] + c] = jnp.zeros((16, 128), BF16)
 
-    def vec_copy(i, d):
+    side = 2 * jnp.bitwise_and(me, 1) - 1
+
+    def vec_copy(role):
+        to = (me + side, me - 2 * side, me - side, me - side)[role]
+        block = (2 - side, 2 + 2 * side, 2 + side, 2 + 2 * side)[role]
+        mine = 2 + side if role == 3 else 2
         return pltpu.make_async_remote_copy(
-            src_ref=vectors_hbm, dst_ref=window.at[pl.ds((2 - d) * 4, 4)],
-            send_sem=vec_send.at[i], recv_sem=vec_recv.at[3 - i],
-            device_id=where_is(me + d), device_id_type=MESH)
+            src_ref=window.at[pl.ds(mine * 4, 4)], dst_ref=window.at[pl.ds(block * 4, 4)],
+            send_sem=vec_send.at[role], recv_sem=vec_recv.at[role],
+            device_id=where_is(to), device_id_type=MESH)
+
+    vec_goes = [inside(me + side), inside(me - 2 * side), inside(me - side), inside(me + side)]
+    vec_comes = [inside(me + side), inside(me + 2 * side), inside(me - side), inside(me - 2 * side)]
 
     def coef_copy(i, d):
         return pltpu.make_async_remote_copy(
@@ -158,6 +166,8 @@
 
     for load in loads[:4]:
         load.wait()
+    for load in loads[4:]:
+        load.start()
     own = [dot_t(window[8 + t], basis[t]).astype(BF16) for t in range(4)]
     coefficients = jnp.concatenate(own, axis=1)
     coeffs[2] = coefficients
@@ -170,15 +180,17 @@
     halves[0, 1] = low
 
     pl.semaphore_wait(barrier, beside)
-    relayed = tell(known.at[0], (-8, 8))
+    below = tell(known.at[1], (-8,))
+    above = tell(known.at[0], (8,))
     swap.start()
     for i, d in enumerate(NEAR_OFFSETS):
         @pl.when(inside(me + d))
         def _():
             coef_copy(i, d).start()
-            vec_copy(i, d).start()
     for slot in range(4):
         send_up(0, slot)
+    for role in range(3):
+        pl.when(vec_goes[role])(vec_copy(role).start)
     swap.wait_recv()
     half = half + (halves[1, 0].astype(F32) + halves[1, 1].astype(F32))
     ups[1] = half.astype(BF16)
@@ -187,9 +199,38 @@
     ups[2] = packed(twice(dot, pair, ltransfer[1, 0]))
     for slot in range(4):
         send_up(1, slot)
-    pl.semaphore_wait(known.at[0], relayed)
-    for slot in (0, 3, 1, 2):
-        send_up(2, slot)
+
+    def send_two_off(slot, c, close):
+        reached = (c <= chip) if slot == 1 else (c >= chip)
+        if c == slot - 1:
+            if not close:
+                return
+            reached = True
+        elif not close:
+            reached = jnp.logical_not(reached)
+        pl.when(both(goes(2, slot), reached))(up_copy(2, slot, c).start)
+
+    def to_above():
+        @pl.when(above > 0)
+        def _():
+            pl.semaphore_wait(known.at[1], above)
+
+        send_up(2, 0)
+        send_two_off(1, 1, False)
+
+    for slot in (1, 2):
+        for c in range(2):
+            send_two_off(slot, c, True)
+    rising = jnp.bitwise_and(jnp.right_shift(me, 2), 7) < 4
+    pl.when(rising)(to_above)
+
+    @pl.when(below > 0)
+    def _():
+        pl.semaphore_wait(known.at[0], below)
+
+    send_up(2, 3)
+    send_two_off(2, 0, False)
+    pl.when(jnp.logical_not(rising))(to_above)
 
     loads[4].wait()
     transfer_all = transfer[...].reshape(256, 64)
@@ -230,6 +271,11 @@
                 for c in range(CHIPS[level]):
                     arrival(level, slot, c).wait_recv()
 
+    @pl.when(vec_comes[0])
+    def _():
+        vec_copy(0).wait_recv()
+        vec_copy(3).start()
+
     for i, d in enumerate(NEAR_OFFSETS):
         pl.when(inside(me - d))(coef_copy(i, d).wait_recv)
 
@@ -262,8 +308,8 @@
     loads[6].wait()
     loads[7].wait()
     loads[8].wait()
-    for i, d in enumerate(NEAR_OFFSETS):
-        pl.when(inside(me - d))(vec_copy(i, d).wait_recv)
+    for role in range(1, 4):
+        pl.when(vec_comes[role])(vec_copy(role).wait_recv)
     for t in range(4):
         picked = []
         for j in range(3):
@@ -279,10 +325,11 @@
         out_ref[t] = out_ref[t] + dot(field[:, t * 64:(t + 1) * 64], basis[t])
 
     swap.wait_send()
+    for role in range(4):
+        pl.when(vec_goes[role])(vec_copy(role).wait_send)
     for i, d in enumerate(NEAR_OFFSETS):
         @pl.when(inside(me + d))
         def _():
-            vec_copy(i, d).wait_send()
             coef_copy(i, d).wait_send()
     for level in range(3):
         for slot in range(4):
@@ -317,7 +364,7 @@
             pltpu.SMEM((4, 3), jnp.int32),
             pltpu.SMEM((4,), jnp.int32),
             pltpu.SMEM((4, 6), jnp.int32),
-            dma((10,)), dma((4,)), dma((4,)), dma((4,)), dma((4,)), dma((16,)), dma((16,)), dma((2,)), pltpu.SemaphoreType.REGULAR((1,)),
+            dma((10,)), dma((4,)), dma((4,)), dma((4,)), dma((4,)), dma((16,)), dma((16,)), dma((2,)), pltpu.SemaphoreType.REGULAR((2,)),
         ],
         compiler_params=pltpu.CompilerParams(
             collective_id=0, has_side_effects=True, vmem_limit_bytes=32 * 2**20),

time: 17.9 us -> 16.9 us (0.944)
  Pallas kernels: 16.9 us -> 16.1 us
    pallas_call x1, Pallas kernels: 16.9 us -> 16.1 us  [on_device(): pl.pallas_call(kernel, out_shape=jax.ShapeDtypeStruct((4, 32, 256), F32),...]
where the time goes in v5:
time: 16.9 us; the launch traced here: 16.7 us
  Pallas kernels  16.1 us (95%)
  local copies, waits for them, and re-layouts  0.66 us (4%)
    pallas_call x1, Pallas kernels, on_device(): pl.pallas_call(kernel, out_shape=jax.ShapeDtypeStruct((4, 32, 256), F32),...  16.1 us
    unnamed x1, local copies, waits for them, and re-layouts  0.66 us

profile of v5, /device:TPU:9, one launch (start us, length us, event | category | flops | bytes accessed | tf_op | source)
XLA Modules:
  0.0 16.7 jit_solution(13483735288030427191)
XLA Ops:
  0.0 16.1 %h2_product.1 = f32[4,32,256]{2,1,0:T(8,128)S(1)} custom-call(s32[4,3]{1,0:T(4,128)} %near_index_hbm.1, s32[4]{0:T(128)} %near_count_hbm.1, s32[4,6]{1,0:T(4,128)} %far_index_hbm.1, bf16[4,32,256]{2,1,0:T(8,128)(2,1)} %vectors_hbm.1, bf16[4,64,256]{2,1,0:T(8,128)(2,1)} %bitcast.1, bf16[4,3,256,256]{3,2,1,0:T(8,128)(2,1)} %near_hbm.1, ...), custom_call_target="tpu_custom_call" | custom-call | tf_op jit(solution)/shard_map/h2_product/pallas_call | solution.py:345
  16.1 0.7 %copy.12 = f32[4,32,256]{2,1,0:T(8,128)} copy(f32[4,32,256]{2,1,0:T(8,128)S(1)} %h2_product.1) | data formatting | bytes 262144

commit v6 on v5

--- a/solution.py
+++ b/solution.py
@@ -8,7 +8,6 @@
 MESH = pl.DeviceIdType.MESH
 NODES = 512
 OFFSETS = (-3, -2, 2, 3)
-NEAR_OFFSETS = (-2, -1, 1, 2)
 F32, BF16 = jnp.float32, jnp.bfloat16
 
 
@@ -60,6 +59,24 @@
 
     def inside(device):
         return jnp.logical_and(device >= 0, device < NODES)
+
+    barrier = pltpu.get_barrier_semaphore()
+
+    def tell(semaphore, distances):
+        count = jnp.int32(0)
+        for d in distances:
+            there = inside(me + d)
+            count = count + (both(there, me + d != 0) if d < 0 else there).astype(jnp.int32)
+            if d > 0 or semaphore is not barrier:
+                there = both(there, (me if d > 0 else me + d) != 0)
+
+            @pl.when(there)
+            def _():
+                pl.semaphore_signal(semaphore, inc=1, device_id=where_is(me + d), device_id_type=MESH)
+
+        return count
+
+    beside = tell(barrier, (-8, 8, -6, 6, -4, 4, -3, 3, -2, 2, -1, 1))
 
     loads = [
         pltpu.make_async_copy(source, target, load_sem.at[i])
@@ -79,22 +96,6 @@
     for load in loads[:4]:
         load.start()
 
-    barrier = pltpu.get_barrier_semaphore()
-
-    def tell(semaphore, distances):
-        count = jnp.int32(0)
-        for d in distances:
-            there = inside(me + d)
-            count = count + there.astype(jnp.int32)
-
-            @pl.when(there)
-            def _():
-                pl.semaphore_signal(semaphore, inc=1, device_id=where_is(me + d), device_id_type=MESH)
-
-        return count
-
-    beside = tell(barrier, (-8, 8, -6, 6, -4, 4, -3, 3, -2, 2, -1, 1))
-
     for level in range(3):
         members = 2**level
         cluster = jnp.right_shift(me, level)
@@ -118,22 +119,27 @@
             device_id=where_is(to), device_id_type=MESH)
 
     vec_goes = [inside(me + side), inside(me - 2 * side), inside(me - side), inside(me + side)]
+    not_first = [me + side != 0, me - 2 * side != 0, me - side != 0]
     vec_comes = [inside(me + side), inside(me + 2 * side), inside(me - side), inside(me - 2 * side)]
 
-    def coef_copy(i, d):
+    def coef_copy(role):
+        to = (me + side, me - 2 * side, me - side, me - side)[role]
+        block = (2 - side, 2 + 2 * side, 2 + side, 2 + 2 * side)[role]
         return pltpu.make_async_remote_copy(
-            src_ref=coeffs.at[2], dst_ref=coeffs.at[2 - d],
-            send_sem=coef_send.at[i], recv_sem=coef_recv.at[3 - i],
-            device_id=where_is(me + d), device_id_type=MESH)
+            src_ref=coeffs.at[2 + side if role == 3 else 2], dst_ref=coeffs.at[block],
+            send_sem=coef_send.at[role], recv_sem=coef_recv.at[role],
+            device_id=where_is(to), device_id_type=MESH)
 
     core, chip = jnp.bitwise_and(me, 1), jnp.bitwise_and(jnp.right_shift(me, 1), 1)
+
+    def up_target(level, slot, c):
+        if level == 2:
+            return (jnp.right_shift(me, 2) - OFFSETS[slot]) * 4 + 2 * c + core
+        return me - OFFSETS[slot] * 2**level
 
     def up_copy(level, slot, c):
         first = FIRST[level] + slot * CHIPS[level]
-        if level == 2:
-            to, mine = (jnp.right_shift(me, 2) - OFFSETS[slot]) * 4 + 2 * c + core, first + chip
-        else:
-            to, mine = me - OFFSETS[slot] * 2**level, first
+        to, mine = up_target(level, slot, c), first + chip if level == 2 else first
         return pltpu.make_async_remote_copy(
             src_ref=ups.at[level], dst_ref=arrived.at[mine],
             send_sem=up_send.at[first + c], recv_sem=up_recv.at[mine],
@@ -162,7 +168,10 @@
         @pl.when(goes(level, slot))
         def _():
             for c in range(CHIPS[level]):
-                up_copy(level, slot, c).start()
+                if OFFSETS[slot] > 0 and c == 0:
+                    pl.when(up_target(level, slot, c) != 0)(up_copy(level, slot, c).start)
+                else:
+                    up_copy(level, slot, c).start()
 
     for load in loads[:4]:
         load.wait()
@@ -182,15 +191,27 @@
     pl.semaphore_wait(barrier, beside)
     below = tell(known.at[1], (-8,))
     above = tell(known.at[0], (8,))
-    swap.start()
-    for i, d in enumerate(NEAR_OFFSETS):
-        @pl.when(inside(me + d))
-        def _():
-            coef_copy(i, d).start()
+
+    @pl.when(me == 0)
+    def _():
+        for device in (1, 2, 3, 4, 6, 8):
+            pl.semaphore_signal(known.at[2], inc=1, device_id=where_is(jnp.int32(device)), device_id_type=MESH)
+
+    pl.when(me != 1)(swap.start)
+    for role in range(3):
+        pl.when(both(vec_goes[role], not_first[role]))(coef_copy(role).start)
     for slot in range(4):
         send_up(0, slot)
     for role in range(3):
-        pl.when(vec_goes[role])(vec_copy(role).start)
+        pl.when(both(vec_goes[role], not_first[role]))(vec_copy(role).start)
+
+    @pl.when(me == 1)
+    def _():
+        pl.semaphore_wait(known.at[2], 1)
+        swap.start()
+        coef_copy(2).start()
+        vec_copy(2).start()
+
     swap.wait_recv()
     half = half + (halves[1, 0].astype(F32) + halves[1, 1].astype(F32))
     ups[1] = half.astype(BF16)
@@ -208,6 +229,7 @@
             reached = True
         elif not close:
             reached = jnp.logical_not(reached)
+        reached = both(reached, up_target(2, slot, c) != 0)
         pl.when(both(goes(2, slot), reached))(up_copy(2, slot, c).start)
 
     def to_above():
@@ -231,6 +253,23 @@
     send_up(2, 3)
     send_two_off(2, 0, False)
     pl.when(jnp.logical_not(rising))(to_above)
+
+    @pl.when(both(both(me >= 2, me <= 14), jnp.logical_or(core == 0, me == 3)))
+    def _():
+        pl.semaphore_wait(known.at[2], 1)
+
+        @pl.when(both(both(me >= 2, me <= 6), core == 0))
+        def _():
+            pl.semaphore_signal(known.at[2], inc=1, device_id=where_is(me + 8), device_id_type=MESH)
+
+        @pl.when(me == 8)
+        def _():
+            pl.semaphore_signal(known.at[1], inc=1, device_id=where_is(jnp.int32(0)), device_id_type=MESH)
+
+        for level in range(3):
+            for slot in (2, 3):
+                pl.when(up_target(level, slot, 0) == 0)(up_copy(level, slot, 0).start)
+
 
     loads[4].wait()
     transfer_all = transfer[...].reshape(256, 64)
@@ -273,11 +312,13 @@
 
     @pl.when(vec_comes[0])
     def _():
+        coef_copy(0).wait_recv()
+        coef_copy(3).start()
         vec_copy(0).wait_recv()
         vec_copy(3).start()
 
-    for i, d in enumerate(NEAR_OFFSETS):
-        pl.when(inside(me - d))(coef_copy(i, d).wait_recv)
+    for role in range(1, 4):
+        pl.when(vec_comes[role])(coef_copy(role).wait_recv)
 
     loads[5].wait()
     loads[9].wait()
@@ -304,6 +345,21 @@
 
     wait_level(0)
     field = field + level_part(0)
+
+    def all_sent(level):
+        for slot in range(4):
+            @pl.when(goes(level, slot))
+            def _():
+                for c in range(CHIPS[level]):
+                    up_copy(level, slot, c).wait_send()
+
+    swap.wait_send()
+    for role in range(4):
+        pl.when(vec_goes[role])(coef_copy(role).wait_send)
+    all_sent(0)
+    all_sent(1)
+    for role in range(3):
+        pl.when(vec_goes[role])(vec_copy(role).wait_send)
 
     loads[6].wait()
     loads[7].wait()
@@ -324,19 +380,8 @@
     for t in range(4):
         out_ref[t] = out_ref[t] + dot(field[:, t * 64:(t + 1) * 64], basis[t])
 
-    swap.wait_send()
-    for role in range(4):
-        pl.when(vec_goes[role])(vec_copy(role).wait_send)
-    for i, d in enumerate(NEAR_OFFSETS):
-        @pl.when(inside(me + d))
-        def _():
-            coef_copy(i, d).wait_send()
-    for level in range(3):
-        for slot in range(4):
-            @pl.when(goes(level, slot))
-            def _():
-                for c in range(CHIPS[level]):
-                    up_copy(level, slot, c).wait_send()
+    pl.when(vec_goes[3])(vec_copy(3).wait_send)
+    all_sent(2)
 
 
 def on_device(vectors, leaf_basis, near_blocks, near_index, near_count, leaf_couple, far_index, leaf_transfer, level_couple, level_transfer):
@@ -364,7 +409,7 @@
             pltpu.SMEM((4, 3), jnp.int32),
             pltpu.SMEM((4,), jnp.int32),
             pltpu.SMEM((4, 6), jnp.int32),
-            dma((10,)), dma((4,)), dma((4,)), dma((4,)), dma((4,)), dma((16,)), dma((16,)), dma((2,)), pltpu.SemaphoreType.REGULAR((2,)),
+            dma((10,)), dma((4,)), dma((4,)), dma((4,)), dma((4,)), dma((16,)), dma((16,)), dma((2,)), pltpu.SemaphoreType.REGULAR((3,)),
         ],
         compiler_params=pltpu.CompilerParams(
             collective_id=0, has_side_effects=True, vmem_limit_bytes=32 * 2**20),

time: 16.9 us -> 16.7 us (0.988)
  the two profiles are of different devices: /device:TPU:9 before, /device:TPU:264 now
where the time goes in v6:
time: 16.7 us; the launch traced here: 16.6 us
  Pallas kernels  15.9 us (95%)
  local copies, waits for them, and re-layouts  0.66 us (4%)
    pallas_call x1, Pallas kernels, on_device(): pl.pallas_call(kernel, out_shape=jax.ShapeDtypeStruct((4, 32, 256), F32),...  15.9 us
    unnamed x1, local copies, waits for them, and re-layouts  0.66 us

profile of v6, /device:TPU:264, one launch (start us, length us, event | category | flops | bytes accessed | tf_op | source)
XLA Modules:
  0.0 16.6 jit_solution(403265341220420863)
XLA Ops:
  0.0 15.9 %h2_product.1 = f32[4,32,256]{2,1,0:T(8,128)S(1)} custom-call(s32[4,3]{1,0:T(4,128)} %near_index_hbm.1, s32[4]{0:T(128)} %near_count_hbm.1, s32[4,6]{1,0:T(4,128)} %far_index_hbm.1, bf16[4,32,256]{2,1,0:T(8,128)(2,1)} %vectors_hbm.1, bf16[4,64,256]{2,1,0:T(8,128)(2,1)} %bitcast.1, bf16[4,3,256,256]{3,2,1,0:T(8,128)(2,1)} %near_hbm.1, ...), custom_call_target="tpu_custom_call" | custom-call | tf_op jit(solution)/shard_map/h2_product/pallas_call | solution.py:390
  15.9 0.7 %copy.12 = f32[4,32,256]{2,1,0:T(8,128)} copy(f32[4,32,256]{2,1,0:T(8,128)S(1)} %h2_product.1) | data formatting | bytes 262144

commit v7 on v6

--- a/solution.py
+++ b/solution.py
@@ -62,11 +62,15 @@
 
     barrier = pltpu.get_barrier_semaphore()
 
-    def tell(semaphore, distances):
+    def one_row(a, b):
+        return jnp.right_shift(me + a, 5) == jnp.right_shift(me + b, 5)
+
+    def tell(semaphore, distances, when=True, comes_when=True):
         count = jnp.int32(0)
         for d in distances:
             there = inside(me + d)
-            count = count + (both(there, me + d != 0) if d < 0 else there).astype(jnp.int32)
+            count = count + both(both(there, me + d != 0) if d < 0 else there, comes_when).astype(jnp.int32)
+            there = both(there, when)
             if d > 0 or semaphore is not barrier:
                 there = both(there, (me if d > 0 else me + d) != 0)
 
@@ -189,8 +193,13 @@
     halves[0, 1] = low
 
     pl.semaphore_wait(barrier, beside)
-    below = tell(known.at[1], (-8,))
-    above = tell(known.at[0], (8,))
+    near_end, near_start = jnp.logical_not(one_row(0, 8)), jnp.logical_not(one_row(0, -8))
+    below = tell(known.at[1], (-8,), one_row(0, -8), one_row(0, -8))
+    below += tell(known.at[1], (-4,), jnp.logical_not(one_row(-4, 4)), near_start)
+    below += tell(known.at[1], (-6,), both(chip == 1, jnp.logical_not(one_row(-6, 2))), both(chip == 1, near_start))
+    above = tell(known.at[0], (8,), one_row(0, 8), one_row(0, 8))
+    above += tell(known.at[0], (4,), jnp.logical_not(one_row(-4, 4)), near_end)
+    above += tell(known.at[0], (6,), both(chip == 0, jnp.logical_not(one_row(6, -2))), both(chip == 0, near_end))
 
     @pl.when(me == 0)
     def _():

time: 16.7 us -> 16.3 us (0.976)
  the two profiles are of different devices: /device:TPU:264 before, /device:TPU:448 now
where the time goes in v7:
time: 16.3 us; the launch traced here: 16.2 us
  Pallas kernels  15.5 us (95%)
  local copies, waits for them, and re-layouts  0.66 us (4%)
    pallas_call x1, Pallas kernels, on_device(): pl.pallas_call(kernel, out_shape=jax.ShapeDtypeStruct((4, 32, 256), F32),...  15.5 us
    unnamed x1, local copies, waits for them, and re-layouts  0.66 us

profile of v7, /device:TPU:448, one launch (start us, length us, event | category | flops | bytes accessed | tf_op | source)
XLA Modules:
  0.0 16.2 jit_solution(5448586723212195266)
XLA Ops:
  0.0 15.5 %h2_product.1 = f32[4,32,256]{2,1,0:T(8,128)S(1)} custom-call(s32[4,3]{1,0:T(4,128)} %near_index_hbm.1, s32[4]{0:T(128)} %near_count_hbm.1, s32[4,6]{1,0:T(4,128)} %far_index_hbm.1, bf16[4,32,256]{2,1,0:T(8,128)(2,1)} %vectors_hbm.1, bf16[4,64,256]{2,1,0:T(8,128)(2,1)} %bitcast.1, bf16[4,3,256,256]{3,2,1,0:T(8,128)(2,1)} %near_hbm.1, ...), custom_call_target="tpu_custom_call" | custom-call | tf_op jit(solution)/shard_map/h2_product/pallas_call | solution.py:399
  15.5 0.7 %copy.12 = f32[4,32,256]{2,1,0:T(8,128)} copy(f32[4,32,256]{2,1,0:T(8,128)S(1)} %h2_product.1) | data formatting | bytes 262144
